TPU v7x, 256 devices: a whole 4x4x8 slice. The times are simulated.
256 devices in a mesh: interval: 8 (over x, y_lo), slab: 32 (over y_hi, z, core).
Axes of the slice: x: 4, y: 4 (y_hi: 2, y_lo: 2; y = y_hi * 2 + y_lo), z: 8, core: 2. Of those that a mesh axis runs over, the one named last changes fastest.
Arguments:
- states: float32 [16, 64, 256, 512], P('interval', 'slab'), may hold values from -0.9 to 0.9
- occupations: int32 [16], P('interval'), may hold values from 1 to 64
- core_density: float32 [64, 256, 512], P('slab'), may hold values from 0.1 to 1
Outputs:
- potential: float32 [64, 256, 512], P('slab', 'interval')
All inputs are finite; a program needn't handle non-finite values.
Results may differ from a plain program's by a relative error of at most 0.00002.
Values sent between devices are 32-bit elements; how exact they have to be, the bound alone decides.
No kernel may reach another device: no remote copies, remote signals or barrier semaphores. Data moves between devices by JAX's collectives and lax.ppermute only.
A program may use at most 64 MiB of HBM per device.

v0:
```python
import jax
import jax.numpy as jnp
from jax import lax
from jax.sharding import PartitionSpec as P

spacing = 0.25
denominator = 64.0
pbe_kappa = 0.804
pbe_mu = 0.2195149727645171
pbe_beta = 0.06672455060314922
pw_alpha = 0.0310907


def with_halo(block, sides, width):
    for axis, dim in sides:
        count = lax.axis_size(axis)
        forward = [(i, i + 1) for i in range(count - 1)]
        forward.append((count - 1, 0))
        backward = [(target, source) for source, target in forward]
        low = lax.ppermute(
            lax.slice_in_dim(block, block.shape[dim] - width, None, axis=dim), axis, forward
        )
        high = lax.ppermute(lax.slice_in_dim(block, 0, width, axis=dim), axis, backward)
        block = jnp.concatenate([low, block, high], axis=dim)
    return block


def deriv_roll(field, axis):
    near = jnp.roll(field, -1, axis) - jnp.roll(field, 1, axis)
    far = jnp.roll(field, -2, axis) - jnp.roll(field, 2, axis)
    return (8.0 * near - far) / (12.0 * spacing)


def deriv_inner(padded, axis):
    count = padded.shape[axis] - 4
    near = lax.slice_in_dim(padded, 3, 3 + count, axis=axis) - lax.slice_in_dim(
        padded, 1, 1 + count, axis=axis
    )
    far = lax.slice_in_dim(padded, 4, 4 + count, axis=axis) - lax.slice_in_dim(
        padded, 0, count, axis=axis
    )
    return (8.0 * near - far) / (12.0 * spacing)


def pbe_energy(density, grad_sq):
    pbe_gamma = (1.0 - jnp.log(2.0)) / jnp.pi**2
    k_fermi = jnp.cbrt(3.0 * jnp.pi**2 * density)
    ex_unif = -0.75 * jnp.cbrt(3.0 / jnp.pi) * jnp.cbrt(density)
    s_sq = grad_sq / (4.0 * k_fermi**2 * density**2)
    f_exch = 1.0 + pbe_kappa - pbe_kappa / (1.0 + pbe_mu * s_sq / pbe_kappa)
    radius = jnp.cbrt(3.0 / (4.0 * jnp.pi * density))
    root_r = jnp.sqrt(radius)
    lower = (
        2.0
        * pw_alpha
        * (7.5957 * root_r + 3.5876 * radius + 1.6382 * radius * root_r + 0.49294 * radius**2)
    )
    e_corr = -2.0 * pw_alpha * (1.0 + 0.2137 * radius) * jnp.log(1.0 + 1.0 / lower)
    k_screen = jnp.sqrt(4.0 * k_fermi / jnp.pi)
    t_sq = grad_sq / (4.0 * k_screen**2 * density**2)
    factor = pbe_beta / pbe_gamma / jnp.expm1(-e_corr / pbe_gamma)
    ratio_t = (1.0 + factor * t_sq) / (1.0 + factor * t_sq + factor**2 * t_sq**2)
    h_term = pbe_gamma * jnp.log(1.0 + pbe_beta / pbe_gamma * t_sq * ratio_t)
    return density * (ex_unif * f_exch + e_corr + h_term)


def local_derivs(density, grad_sq):
    return jax.grad(lambda rho, grd: jnp.sum(pbe_energy(rho, grd)), argnums=(0, 1))(
        density, grad_sq
    )


def planes_deriv(flux_z):
    padded = with_halo(flux_z, (("slab", 0),), 2)
    return deriv_inner(padded, 0)


def shards(states, occupations, core_density):
    weights = occupations.astype(jnp.float32) / denominator
    terms = weights[0] * states[0] * states[0]
    terms = terms + weights[1] * states[1] * states[1]
    density = lax.psum(terms, "interval") + core_density
    padded = with_halo(density, (("slab", 0),), 2)
    grad_z = deriv_inner(padded, 0)
    grad_x = deriv_roll(density, 1)
    grad_y = deriv_roll(density, 2)
    grad_sq = grad_z * grad_z + grad_x * grad_x + grad_y * grad_y
    energy_rho, energy_grad = local_derivs(density, grad_sq)
    diverge = (
        planes_deriv(2.0 * energy_grad * grad_z)
        + deriv_roll(2.0 * energy_grad * grad_x, 1)
        + deriv_roll(2.0 * energy_grad * grad_y, 2)
    )
    whole_field = energy_rho - diverge
    width = whole_field.shape[1] // lax.axis_size("interval")
    return lax.dynamic_slice_in_dim(whole_field, lax.axis_index("interval") * width, width, 1)


def solution(mesh):
    return jax.shard_map(
        shards,
        mesh=mesh,
        in_specs=(P("interval", "slab", None, None), P("interval"), P("slab", None, None)),
        out_specs=P("slab", "interval", None),
        check_vma=False,
    )
```

profile of v0, /device:TPU:225, one launch (start us, length us, event | category | flops | bytes accessed | tf_op | source)
XLA Modules:
  0.0 166.3 jit_solution(4103295734114470469)
XLA Ops:
  6.5 0.0 all-reduce.2.cloned.1.call-start
  6.5 0.7 convert_multiply_fusion
  7.2 0.6 fusion.65
  7.8 0.0 copy-start
  7.8 4.2 %fusion = f32[2,256,512]{2,1,0:T(8,128)} fusion(f32[2,2,256,512]{3,2,1,0:T(8,128)} %param.3, f32[]{:T(128)} %bitcast.2, f32[]{:T(128)} %bitcast), kind=kLoop, calls=%fused_computation.2 | loop fusion | flops 1310720 | bytes 3145736 | tf_op jit(solution)/shard_map/add | solution.py:81
  12.0 0.0 all-reduce.2.cloned.1.call-update
  12.0 79.0 %all-reduce.2.cloned.1.call-done = f32[2,256,512]{2,1,0:T(8,128)} async-done(((f32[2,256,512]{2,1,0:T(8,128)}), f32[2,256,512]{2,1,0:T(8,128)}) %all-reduce.2.cloned.1.call-update) | async-done | bytes 1048592 | tf_op jit(solution)/shard_map/psum | solution.py:82
  91.0 0.0 copy-done
  91.0 2.1 %broadcast_multiply_fusion.1 = (f32[2,256,512]{2,1,0:T(8,128)S(1)}, f32[2,256,512]{2,1,0:T(8,128)S(1)}) fusion(f32[2,256,512]{2,1,0:T(8,128)} %all-reduce.2.cloned.1.call-done, f32[2,256,512]{2,1,0:T(8,128)S(1)} %copy-done), kind=kLoop, calls=%fused_computation.71 | loop fusion | flops 1048576 | bytes 4194304 | tf_op jit(solution)/shard_map/jvp()/mul | solution.py:49
  93.2 0.1 fusion.60
  93.3 0.1 fusion.58
  93.5 6.8 %collective-permute-start.1 = (f32[2,256,512]{2,1,0:T(8,128)S(1)}, f32[2,256,512]{2,1,0:T(8,128)S(1)}, u32[]{:S(2)}, u32[]{:S(2)}) collective-permute-start(f32[2,256,512]{2,1,0:T(8,128)S(1)} %get-tuple-element.12), channel_id=1, source_target_pairs={{0,1},{1,2},{2,3},{3,4},{4,5},{5,6},{6,7},{7,8},{8,9},{9,10},{10,1... | collective-permute-start | bytes 3145736 | tf_op jit(solution)/shard_map/ppermute | solution.py:20
  100.3 0.0 collective-permute-start
  100.3 0.4 fusion.57
  100.7 0.4 fusion.59
  101.1 0.2 fusion.63
  101.3 0.2 fusion.61
  101.6 10.5 %collective-permute-done.1 = f32[2,256,512]{2,1,0:T(8,128)S(1)} collective-permute-done((f32[2,256,512]{2,1,0:T(8,128)S(1)}, f32[2,256,512]{2,1,0:T(8,128)S(1)}, u32[]{:S(2)}, u32[]{:S(2)}) %collective-permute-start.1) | collective-permute-done | bytes 1048608 | tf_op jit(solution)/shard_map/ppermute | solution.py:20
  112.1 6.1 %collective-permute-done = f32[2,256,512]{2,1,0:T(8,128)S(1)} collective-permute-done((f32[2,256,512]{2,1,0:T(8,128)S(1)}, f32[2,256,512]{2,1,0:T(8,128)S(1)}, u32[]{:S(2)}, u32[]{:S(2)}) %collective-permute-start) | collective-permute-done | bytes 1048608 | tf_op jit(solution)/shard_map/ppermute | solution.py:23
  118.2 7.4 %multiply_add_fusion.1 = (f32[2,256,512]{2,1,0:T(8,128)S(1)}, f32[2,256,512]{2,1,0:T(8,128)S(1)}, f32[2,256,512]{2,1,0:T(8,128)S(1)}, f32[2,256,512]{2,1,0:T(8,128)S(1)}) fusion(f32[2,256,512]{2,1,0:T(8,128)S(1)} %get-tuple-element.12, f32[2,256,512]{2,1,0:T(8,128)S(1)} %collective-permute-done, f32[2,256,512]{2,1,0:T(8,128)S(1)} %collective-permute-done.1, ...), kind=kLoop, calls=%fused_computation.46 | loop fusion | flops 21233664 | bytes 15728640 | tf_op jit(solution)/shard_map/jvp()/add | solution.py:64
  125.6 4.9 %multiply_multiply_fusion.3 = (f32[2,256,512]{2,1,0:T(8,128)S(1)}, f32[2,256,512]{2,1,0:T(8,128)S(1)}) fusion(f32[2,256,512]{2,1,0:T(8,128)S(1)} %get-tuple-element.12, f32[2,256,512]{2,1,0:T(8,128)S(1)} %get-tuple-element.6), kind=kLoop, calls=%fused_computation.41 | loop fusion | flops 17039360 | bytes 4194304 | tf_op jit(solution)/shard_map/transpose(jvp())/mul | solution.py:60
  130.5 8.9 %multiply_multiply_fusion.2 = (f32[2,256,512]{2,1,0:T(8,128)S(1)}, f32[2,256,512]{2,1,0:T(8,128)S(1)}, f32[2,256,512]{2,1,0:T(8,128)S(1)}, f32[2,256,512]{2,1,0:...) fusion(f32[2,256,512]{2,1,0:T(8,128)S(1)} %get-tuple-element.12, ...), kind=kLoop, calls=%fused_computation.36 | loop fusion | flops 38010880 | bytes 16777216 | tf_op jit(solution)/shard_map/transpose(jvp())/mul | solution.py:49
  139.4 0.3 fusion.52
  139.8 0.1 fusion.55
  140.0 0.1 fusion.53
  140.1 0.1 collective-permute-start.3
  140.2 0.5 collective-permute-start.2
  140.7 0.2 fusion.49
  141.0 0.3 maximum_subtract_fusion.4
  141.2 0.2 fusion.51
  141.5 0.4 fusion.56
  141.8 0.4 fusion.54
  142.2 9.7 %collective-permute-done.3 = f32[2,256,512]{2,1,0:T(8,128)S(1)} collective-permute-done((f32[2,256,512]{2,1,0:T(8,128)S(1)}, f32[2,256,512]{2,1,0:T(8,128)S(1)}, u32[]{:S(2)}, u32[]{:S(2)}) %collective-permute-start.3) | collective-permute-done | bytes 1048608 | tf_op jit(solution)/shard_map/ppermute | solution.py:20
  152.0 6.2 %collective-permute-done.2 = f32[2,256,512]{2,1,0:T(8,128)S(1)} collective-permute-done((f32[2,256,512]{2,1,0:T(8,128)S(1)}, f32[2,256,512]{2,1,0:T(8,128)S(1)}, u32[]{:S(2)}, u32[]{:S(2)}) %collective-permute-start.2) | collective-permute-done | bytes 1048608 | tf_op jit(solution)/shard_map/ppermute | solution.py:23
  158.1 0.2 fusion.1
  158.3 1.1 fusion.21
  (4 shorter events, 0.0 us)
Async XLA Ops:
  6.5 84.5 %all-reduce.2.cloned.1.call-start = ((), (), s32[]{:S(2)}) async-start(), calls=%async_computation | async-start | bytes 2097152 | tf_op jit(solution)/shard_map/psum | solution.py:82
  7.8 83.2 %copy-start = (f32[2,256,512]{2,1,0:T(8,128)S(1)}, f32[2,256,512]{2,1,0:T(8,128)}, u32[]{:S(2)}) copy-start(f32[2,256,512]{2,1,0:T(8,128)} %param.5) | copy-start | bytes 3145732
  93.5 18.6 %collective-permute-start.1 = (f32[2,256,512]{2,1,0:T(8,128)S(1)}, f32[2,256,512]{2,1,0:T(8,128)S(1)}, u32[]{:S(2)}, u32[]{:S(2)}) collective-permute-start(f32[2,256,512]{2,1,0:T(8,128)S(1)} %get-tuple-element.12), channel_id=1, source_target_pairs={{0,1},{1,2},{2,3},{3,4},{4,5},{5,6},{6,7},{7,8},{8,9},{9,10},{10,1... | collective-permute-start | bytes 3145736 | tf_op jit(solution)/shard_map/ppermute | solution.py:20
  100.3 17.8 %collective-permute-start = (f32[2,256,512]{2,1,0:T(8,128)S(1)}, f32[2,256,512]{2,1,0:T(8,128)S(1)}, u32[]{:S(2)}, u32[]{:S(2)}) collective-permute-start(f32[2,256,512]{2,1,0:T(8,128)S(1)} %get-tuple-element.12), channel_id=1, source_target_pairs={{1,0},{2,1},{3,2},{4,3},{5,4},{6,5},{7,6},{8,7},{9,8},{10,9},{11,1... | collective-permute-start | bytes 3145736 | tf_op jit(solution)/shard_map/ppermute | solution.py:23
  140.1 11.8 %collective-permute-start.3 = (f32[2,256,512]{2,1,0:T(8,128)S(1)}, f32[2,256,512]{2,1,0:T(8,128)S(1)}, u32[]{:S(2)}, u32[]{:S(2)}) collective-permute-start(f32[2,256,512]{2,1,0:T(8,128)S(1)} %get-tuple-element.22), channel_id=1, source_target_pairs={{0,1},{1,2},{2,3},{3,4},{4,5},{5,6},{6,7},{7,8},{8,9},{9,10},{10,1... | collective-permute-start | bytes 3145736 | tf_op jit(solution)/shard_map/ppermute | solution.py:20
  140.2 17.9 %collective-permute-start.2 = (f32[2,256,512]{2,1,0:T(8,128)S(1)}, f32[2,256,512]{2,1,0:T(8,128)S(1)}, u32[]{:S(2)}, u32[]{:S(2)}) collective-permute-start(f32[2,256,512]{2,1,0:T(8,128)S(1)} %get-tuple-element.22), channel_id=1, source_target_pairs={{1,0},{2,1},{3,2},{4,3},{5,4},{6,5},{7,6},{8,7},{9,8},{10,9},{11,1... | collective-permute-start | bytes 3145736 | tf_op jit(solution)/shard_map/ppermute | solution.py:23
Sparse Core Ops, SparseCore 0:
  12.1 78.8 all-reduce.1
where the time goes:
time: 166 us
  waiting for transfers between devices  111 us (67%)
  other arithmetic  30.2 us (18%)
  between operations  13.6 us (8%)
  starting transfers between devices  7.41 us (4%)
  local copies, waits for them, and re-layouts  3.66 us (2%)
    psum x1, waiting for transfers between devices, shards(): density = lax.psum(terms, 'interval') + core_density  79 us
    ppermute x2, waiting for transfers between devices, with_halo(): lax.ppermute(lax.slice_in_dim(block, block.shape[dim] - width, None, axis...  20.2 us
    ppermute x2, waiting for transfers between devices, with_halo(): lax.ppermute(lax.slice_in_dim(block, 0, width, axis=dim), axis, backward)  12.3 us
    mul x2, other arithmetic, pbe_energy(): s_sq = grad_sq / (4.0 * k_fermi ** 2 * density ** 2)  11.1 us
    add x1, other arithmetic, pbe_energy(): return density * (ex_unif * f_exch + e_corr + h_term)  7.43 us
    ppermute x2, starting transfers between devices, with_halo(): lax.ppermute(lax.slice_in_dim(block, block.shape[dim] - width, None, axis...  6.91 us
    mul x1, other arithmetic, pbe_energy(): t_sq = grad_sq / (4.0 * k_screen ** 2 * density ** 2)  4.91 us
    add x1, other arithmetic, shards(): terms = terms + weights[1] * states[1] * states[1]  4.16 us
  transfers between devices with their start and end apart: 5, of which 5 were waited for; matrix products, arithmetic and copies ran while one was open for 2% of the time, Pallas kernels for 0%

commit v1 on v0

v1 whole, which is shorter than its diff:
```python
import functools
import math

import jax
import jax.numpy as jnp
from jax import lax
from jax.experimental import pallas as pl
from jax.experimental.pallas import tpu as pltpu
from jax.sharding import PartitionSpec as P

spacing = 0.25
denominator = 64.0
kappa = 0.804
mu = 0.2195149727645171
beta = 0.06672455060314922
gamma = (1.0 - math.log(2.0)) / math.pi**2
pw_a = 0.0310907
alpha1 = 0.2137
beta_over_gamma = beta / gamma
exch = 0.75 * (3.0 / math.pi) ** (1.0 / 3.0)
rs_unit = (3.0 / (4.0 * math.pi)) ** (1.0 / 3.0)
s_unit = 1.0 / (4.0 * (3.0 * math.pi**2) ** (2.0 / 3.0))
t_unit = math.pi / (16.0 * (3.0 * math.pi**2) ** (1.0 / 3.0))
q1 = 2.0 * pw_a * 7.5957 * rs_unit**0.5
q2 = 2.0 * pw_a * 3.5876 * rs_unit
q3 = 2.0 * pw_a * 1.6382 * rs_unit**1.5
q4 = 2.0 * pw_a * 0.49294 * rs_unit**2

third = 1.0 / (12.0 * spacing)
HALO = 4
VMEM_LIMIT = 40 * 1024 * 1024


def of_density(n, with_energy):
    w = jnp.exp(jnp.log(n) * (-1.0 / 6.0))
    q = w * (q1 + w * (q2 + w * (q3 + w * q4)))
    radius = rs_unit * (w * w)
    slope = 1.0 + alpha1 * radius
    log_term = jnp.log(1.0 + 1.0 / q)
    e_corr = (-2.0 * pw_a) * slope * log_term
    grown = jnp.exp(e_corr * (-1.0 / gamma))
    less = 1.0 / (grown - 1.0)
    factor = beta_over_gamma * less
    if not with_energy:
        return w, factor
    rq = w * (0.5 * q1 + w * (q2 + w * (1.5 * q3 + w * (2.0 * q4))))
    change = (2.0 * pw_a / 3.0) * (alpha1 * radius * log_term - slope * rq / (q * (q + 1.0)))
    return w, factor, e_corr + change, change * factor * (grown * less) * (1.0 / gamma)


def of_gradient(w, factor, g, energy=None):
    w2 = w * w
    w4 = w2 * w2
    w8 = w4 * w4
    s_sq = (s_unit * g) * (w8 * w8)
    t_sq = (t_unit * g) * (w8 * w4 * w2)
    u = factor * t_sq
    up = 1.0 + u
    d = up + u * u
    wide = d + beta_over_gamma * t_sq * up
    inv = 1.0 / (d * wide)
    h_t = beta * (1.0 + 2.0 * u) * inv
    inv_x = 1.0 / (1.0 + (mu / kappa) * s_sq)
    f_s = mu * inv_x * inv_x
    twice = (2.0 * w8) * (t_unit * h_t - (exch * s_unit) * f_s)
    if energy is None:
        return twice
    n, base, change = energy
    h = gamma * jnp.log(wide * wide * inv)
    h_a = -beta * (t_sq * t_sq) * u * (2.0 + u) * inv
    f_x = (1.0 + kappa) - kappa * inv_x
    e_n = base + h + change * h_a - (7.0 / 3.0) * t_sq * h_t
    e_n = e_n - (4.0 / 3.0 * exch) * (n * w4) * (f_x - 2.0 * s_sq * f_s)
    return twice, e_n


def roll(v, shift, axis):
    return pltpu.roll(v, shift % v.shape[axis], axis)


def d_along(v, axis):
    near = roll(v, -1, axis) - roll(v, 1, axis)
    far = roll(v, -2, axis) - roll(v, 2, axis)
    return (8.0 * third) * near - third * far


def d_z(p2, p1, m1, m2):
    return (8.0 * third) * (p1 - m1) - third * (p2 - m2)


def terms_kernel(occ_ref, states_ref, core_ref, out_ref, held, core_held, sems):
    rows = held.shape[2]
    parts, _, wide, _ = out_ref.shape
    own = rows // parts
    pieces = sems.shape[0] - 3
    per = rows // pieces
    me = lax.axis_index("interval")
    flip = lax.rem(lax.axis_index("slab"), 2)
    copies = []
    for k in range(pieces):
        at = pl.ds(k * per, per)
        copies.append(pltpu.make_async_copy(states_ref.at[:, :, at], held.at[:, :, at], sems.at[k]))
    low = pl.multiple_of(lax.rem(me * own + rows - 8, rows), 8)
    mid = pl.multiple_of(me * own, 8)
    top = pl.multiple_of(lax.rem(me * own + own, rows), 8)
    for k, (start, size, to) in enumerate(((low, 8, 0), (mid, own, 8), (top, 8, own + 8))):
        copies.append(
            pltpu.make_async_copy(
                core_ref.at[:, pl.ds(start, size)], core_held.at[:, pl.ds(to, size)], sems.at[pieces + k]
            )
        )
    for c in copies:
        c.start()
    w0 = occ_ref[0].astype(jnp.float32) * (1.0 / denominator)
    w1 = occ_ref[1].astype(jnp.float32) * (1.0 / denominator)
    for k in range(pieces):
        copies[k].wait()
        for i in range(k * per // own, (k + 1) * per // own):
            for p in range(2):
                to = p ^ flip
                for r in range(0, own, 8):
                    a = held[0, p, pl.ds(i * own + r, 8)]
                    b = held[1, p, pl.ds(i * own + r, 8)]
                    t = w0 * a * a + w1 * b * b
                    out_ref[i, to, pl.ds(r + HALO, 8)] = t
                    if r == 0:
                        out_ref[(i - 1) % parts, to, pl.ds(own + HALO, HALO)] = t[:HALO]
                    if r == own - 8:
                        out_ref[(i + 1) % parts, to, pl.ds(0, HALO)] = t[8 - HALO:]
    for c in copies[pieces:]:
        c.wait()
    for p in range(2):
        to = p ^ flip
        out_ref[me, to] = out_ref[me, to] + core_held[p, pl.ds(8 - HALO, wide)]


def density_kernel(s_ref, w_ref, a_ref, base_ref, change_ref, gx_ref, gy_ref):
    rows, cols = s_ref.shape[1:]
    for p in range(2):
        for c in range(0, cols, 128):
            at = pl.ds(c, 128)
            gx_ref[p, :, at] = d_along(s_ref[p, :, at], 0)
        for r in range(0, rows, 8):
            at = pl.ds(r, 8)
            n = s_ref[p, at]
            gy_ref[p, at] = d_along(n, 1)
            w_ref[p, at], a_ref[p, at], base_ref[p, at], change_ref[p, at] = of_density(n, True)


def own_kernel(s_ref, n_ref, w_ref, a_ref, gx_ref, gy_ref, fz_ref, g_ref, twice_ref):
    rows = s_ref.shape[1]
    for r in range(0, rows, 8):
        at = pl.ds(r, 8)
        s = [s_ref[k, at] for k in range(4)]
        n = [n_ref[k, at] for k in range(2)]
        for p, gz in ((0, d_z(s[2], s[1], n[0], n[1])), (1, d_z(s[3], s[2], s[0], n[0]))):
            gx, gy = gx_ref[p, at], gy_ref[p, at]
            g = gz * gz + gx * gx + gy * gy
            twice = of_gradient(w_ref[p, at], a_ref[p, at], g)
            fz_ref[p, at] = twice * gz
            g_ref[p, at] = g
            twice_ref[p, at] = twice


def near_kernel(s_ref, n_ref, w_ref, a_ref, base_ref, change_ref, gx_ref, gy_ref, fz_ref, g_ref, twice_ref, out_ref, gxn, fzn, part):
    rows, cols = s_ref.shape[1:]
    own = rows - 2 * HALO
    for p in range(2):
        for c in range(0, cols, 128):
            at = pl.ds(c, 128)
            gxn[p, :, at] = d_along(n_ref[p, :, at], 0)
            part[p, :, at] = d_along(gx_ref[p, :, at] * twice_ref[p, :, at], 0)
    for r in range(0, rows, 8):
        at = pl.ds(r, 8)
        s = [s_ref[k, at] for k in range(2)]
        n = [n_ref[k, at] for k in range(4)]
        f = []
        for p, gz in ((0, d_z(s[1], s[0], n[1], n[2])), (1, d_z(s[0], n[0], n[2], n[3]))):
            gx, gy = gxn[p, at], d_along(n[p], 1)
            g = gz * gz + gx * gx + gy * gy
            w, factor = of_density(n[p], False)
            f.append(of_gradient(w, factor, g) * gz)
        f0, f1 = fz_ref[0, at], fz_ref[1, at]
        dz = (third * (8.0 * (f1 - f[0]) + f[1]), third * (f[0] - 8.0 * f0))
        for p in range(2):
            twice, e_n = of_gradient(
                w_ref[p, at], a_ref[p, at], g_ref[p, at], (s[p], base_ref[p, at], change_ref[p, at])
            )
            dy = d_along(twice_ref[p, at] * gy_ref[p, at], 1)
            part[p, at] = e_n - (dz[p] + part[p, at] + dy)
    for p in range(2):
        out_ref[p] = part[p, pl.ds(HALO, own)]


def last_kernel(part_ref, fz_ref, out_ref):
    own = part_ref.shape[1]
    flip = lax.rem(lax.axis_index("slab"), 2)
    f0, f1 = fz_ref[0, pl.ds(HALO, own)], fz_ref[1, pl.ds(HALO, own)]
    out_ref[flip] = part_ref[0] - third * f1
    out_ref[1 - flip] = part_ref[1] - third * (f0 - 8.0 * f1)


def call(kernel, outs, *args, scratch=(), specs=None, out_hbm=False):
    f32 = jnp.float32
    if specs is None:
        specs = [pl.BlockSpec(memory_space=pltpu.VMEM)] * len(args)
        args = [pltpu.with_memory_space_constraint(a, pltpu.VMEM) for a in args]
    out_shape = [jax.ShapeDtypeStruct(o, f32) if out_hbm else pltpu.VMEM(o, f32) for o in outs]
    got = pl.pallas_call(
        kernel,
        out_shape=out_shape,
        in_specs=specs,
        out_specs=[pl.BlockSpec(memory_space=pltpu.VMEM)] * len(outs),
        scratch_shapes=list(scratch),
        compiler_params=pltpu.CompilerParams(vmem_limit_bytes=VMEM_LIMIT),
        name=kernel.__name__,
    )(*args)
    return got


def shards(states, occupations, core_density):
    f32 = jnp.float32
    parts = lax.axis_size("interval")
    slabs = lax.axis_size("slab")
    planes, rows, cols = core_density.shape
    own = rows // parts
    wide = own + 2 * HALO
    block = (planes, wide, cols)
    (terms,) = call(
        terms_kernel,
        [(parts, *block)],
        occupations,
        states,
        core_density,
        specs=[pl.BlockSpec(memory_space=pltpu.SMEM), pl.BlockSpec(memory_space=pl.ANY), pl.BlockSpec(memory_space=pl.ANY)],
        scratch=[
            pltpu.VMEM(states.shape, f32),
            pltpu.VMEM((planes, own + 16, cols), f32),
            pltpu.SemaphoreType.DMA((4 + 3,)),
        ],
    )
    density = jnp.sum(lax.all_to_all(terms, "interval", 0, 0), axis=0)
    mates = [(i, i ^ 1) for i in range(slabs)]
    outer = [(i, (i + (1 if i % 2 else -1)) % slabs) for i in range(slabs)]
    mate = lax.ppermute(density, "slab", mates)
    pair = jnp.concatenate([density, mate[::-1]], axis=0)
    beside = lax.ppermute(pair, "slab", outer)
    w, factor, base, change, gx, gy = call(density_kernel, [block] * 6, pair)
    fz, g, twice = call(own_kernel, [block] * 3, pair, beside, w, factor, gx, gy)
    fz_mate = lax.ppermute(fz, "slab", mates)
    (part,) = call(
        near_kernel, [(planes, own, cols)], pair, beside, w, factor, base, change, gx, gy, fz, g, twice,
        scratch=[pltpu.VMEM(block, f32)] * 3,
    )
    (out,) = call(last_kernel, [(planes, own, cols)], part, fz_mate, out_hbm=True)
    return out


def solution(mesh):
    return jax.shard_map(
        shards,
        mesh=mesh,
        in_specs=(P("interval", "slab", None, None), P("interval"), P("slab", None, None)),
        out_specs=P("slab", "interval", None),
        check_vma=False,
    )
```

time: 166 us -> 46.1 us (0.28)
  the two profiles are of different devices: /device:TPU:225 before, /device:TPU:1 now
where the time goes in v1:
time: 46.1 us; the launch traced here: 45.9 us
  blocking collectives  22.8 us (49%)
  starting transfers between devices  10.5 us (23%)
  waiting for transfers between devices  5.4 us (12%)
  Pallas kernels  3.5 us (8%)
  local copies, waits for them, and re-layouts  3.48 us (8%)
    all_to_all x1, blocking collectives, shards(): density = jnp.sum(lax.all_to_all(terms, 'interval', 0, 0), axis=0)  22.8 us
    ppermute x1, starting transfers between devices, shards(): fz_mate = lax.ppermute(fz, 'slab', mates)  6.5 us
    ppermute x1, waiting for transfers between devices, shards(): beside = lax.ppermute(pair, 'slab', outer)  4.37 us
    pallas_call x5, Pallas kernels, call(): pl.pallas_call(kernel, out_shape=out_shape, in_specs=specs, out_specs=[pl...  3.5 us
    unnamed x6, local copies, waits for them, and re-layouts  3.47 us
    ppermute x1, starting transfers between devices, shards(): mate = lax.ppermute(density, 'slab', mates)  2.03 us
    ppermute x1, starting transfers between devices, shards(): beside = lax.ppermute(pair, 'slab', outer)  1.98 us
    ppermute x1, waiting for transfers between devices, shards(): mate = lax.ppermute(density, 'slab', mates)  1.03 us
  transfers between devices with their start and end apart: 3, of which 2 were waited for; matrix products, arithmetic and copies ran while one was open for 0% of the time, Pallas kernels for 3%

profile of v1, /device:TPU:1, one launch (start us, length us, event | category | flops | bytes accessed | tf_op | source)
XLA Modules:
  0.0 45.9 jit_solution(3986786949248692122)
XLA Ops:
  0.0 0.0 copy-start
  0.0 1.6 %copy-done = f32[2,2,256,512]{3,2,1,0:T(8,128)S(1)} copy-done((f32[2,2,256,512]{3,2,1,0:T(8,128)S(1)}, f32[2,2,256,512]{3,2,1,0:T(8,128)}, u32[]{:S(2)}) %copy-start) | copy-done | bytes 2097176
  1.6 0.0 copy-start.1
  1.6 1.2 %copy-done.1 = f32[2,256,512]{2,1,0:T(8,128)S(1)} copy-done((f32[2,256,512]{2,1,0:T(8,128)S(1)}, f32[2,256,512]{2,1,0:T(8,128)}, u32[]{:S(2)}) %copy-start.1) | copy-done | bytes 1048600
  2.8 0.0 copy-start.2
  2.8 0.7 %copy-done.2 = s32[2]{0:T(128)S(1)} copy-done((s32[2]{0:T(128)S(1)}, s32[2]{0:T(128)}, u32[]{:S(2)}) %copy-start.2) | copy-done | bytes 32
  3.5 1.2 %terms_kernel.1 = f32[8,2,40,512]{3,2,1,0:T(8,128)S(1)} custom-call(s32[2]{0:T(128)S(1)} %copy-done.2, f32[2,2,256,512]{3,2,1,0:T(8,128)S(1)} %copy-done, f32[2,256,512]{2,1,0:T(8,128)S(1)} %copy-done.1), custom_call_target="tpu_custom_call" | custom-call | tf_op jit(solution)/shard_map/terms_kernel/pallas_call | solution.py:209
  4.6 22.8 %all_to_all.5 = f32[8,2,40,512]{3,2,1,0:T(8,128)S(1)} all-to-all(f32[8,2,40,512]{3,2,1,0:T(8,128)S(1)} %terms_kernel.1), channel_id=1, replica_groups=mesh['interval'=8,'slab'=32] {'interval'}, dimensions={0} | all-to-all | bytes 2621440 | tf_op jit(solution)/shard_map/all_to_all | solution.py:242
  27.5 0.1 reduce_sum.9
  27.6 2.0 %collective-permute-start = (f32[2,40,512]{2,1,0:T(8,128)S(1)}, f32[2,40,512]{2,1,0:T(8,128)S(1)}, u32[]{:S(2)}, u32[]{:S(2)}) collective-permute-start(f32[2,40,512]{2,1,0:T(8,128)S(1)} %reduce_sum.9), channel_id=1, source_target_pairs={{0,1},{1,0},{2,3},{3,2},{4,5},{5,4},{6,7},{7,6},{8,9},{9,8},{10,11... | collective-permute-start | bytes 491528 | tf_op jit(solution)/shard_map/ppermute | solution.py:245
  29.6 1.0 %collective-permute-done = f32[2,40,512]{2,1,0:T(8,128)S(1)} collective-permute-done((f32[2,40,512]{2,1,0:T(8,128)S(1)}, f32[2,40,512]{2,1,0:T(8,128)S(1)}, u32[]{:S(2)}, u32[]{:S(2)}) %collective-permute-start) | collective-permute-done | bytes 163872 | tf_op jit(solution)/shard_map/ppermute | solution.py:245
  30.7 2.0 %collective-permute-start.1 = (f32[4,40,512]{2,1,0:T(8,128)S(1)}, f32[4,40,512]{2,1,0:T(8,128)S(1)}, u32[]{:S(2)}, u32[]{:S(2)}) collective-permute-start(f32[4,40,512]{2,1,0:T(8,128)S(1)} %pad_maximum_fusion.s_ref), channel_id=1, source_target_pairs={{0,31},{1,2},{2,1},{3,4},{4,3},{5,6},{6,5},{7,8},{8,7},{9,10},{10,... | collective-permute-start | bytes 983048 | tf_op jit(solution)/shard_map/ppermute | solution.py:247
  32.7 0.4 density_kernel.1
  33.0 4.4 %collective-permute-done.1.n_ref = f32[4,40,512]{2,1,0:T(8,128)S(1)} collective-permute-done((f32[4,40,512]{2,1,0:T(8,128)S(1)}, f32[4,40,512]{2,1,0:T(8,128)S(1)}, u32[]{:S(2)}, u32[]{:S(2)}) %collective-permute-start.1) | collective-permute-done | bytes 327712 | tf_op jit(solution)/shard_map/ppermute | solution.py:247
  37.4 0.2 own_kernel.1
  37.7 6.5 %collective-permute-start.2 = (f32[2,40,512]{2,1,0:T(8,128)S(1)}, f32[2,40,512]{2,1,0:T(8,128)S(1)}, u32[]{:S(2)}, u32[]{:S(2)}) collective-permute-start(f32[2,40,512]{2,1,0:T(8,128)S(1)} %get-tuple-element.20.fz_ref), channel_id=1, source_target_pairs={{0,1},{1,0},{2,3},{3,2},{4,5},{5,4},{6,7},{7,6},{8,9},{9,8},{10,11... | collective-permute-start | bytes 491528 | tf_op jit(solution)/shard_map/ppermute | solution.py:250
  44.2 1.0 %near_kernel.1.part_ref = f32[2,32,512]{2,1,0:T(8,128)S(1)} custom-call(f32[4,40,512]{2,1,0:T(8,128)S(1)} %pad_maximum_fusion.s_ref, f32[4,40,512]{2,1,0:T(8,128)S(1)} %collective-permute-done.1.n_ref, f32[2,40,512]{2,1,0:T(8,128)S(1)} %get-tuple-element.14.w_ref, f32[2,40,512]{2,1,0:T(8,128)S(1)} %get-tuple-element.15.a_ref, ...), custom_call_target="tpu_custom_call" | custom-call | tf_op jit(solution)/shard_map/near_kernel/pallas_call | solution.py:209
  45.2 0.0 collective-permute-done.2.fz_ref
  45.2 0.7 %last_kernel.1 = f32[2,32,512]{2,1,0:T(8,128)} custom-call(f32[2,32,512]{2,1,0:T(8,128)S(1)} %near_kernel.1.part_ref, f32[2,40,512]{2,1,0:T(8,128)S(1)} %collective-permute-done.2.fz_ref), custom_call_target="tpu_custom_call" | custom-call | tf_op jit(solution)/shard_map/last_kernel/pallas_call | solution.py:209
  (2 shorter events, 0.0 us)
Async XLA Ops:
  0.0 1.6 %copy-start = (f32[2,2,256,512]{3,2,1,0:T(8,128)S(1)}, f32[2,2,256,512]{3,2,1,0:T(8,128)}, u32[]{:S(2)}) copy-start(f32[2,2,256,512]{3,2,1,0:T(8,128)} %states_ref.1) | copy-start | bytes 6291460
  1.6 1.2 %copy-start.1 = (f32[2,256,512]{2,1,0:T(8,128)S(1)}, f32[2,256,512]{2,1,0:T(8,128)}, u32[]{:S(2)}) copy-start(f32[2,256,512]{2,1,0:T(8,128)} %core_ref.1) | copy-start | bytes 3145732
  2.8 0.7 %copy-start.2 = (s32[2]{0:T(128)S(1)}, s32[2]{0:T(128)}, u32[]{:S(2)}) copy-start(s32[2]{0:T(128)} %occ_ref.1) | copy-start | bytes 28
  27.6 3.1 %collective-permute-start = (f32[2,40,512]{2,1,0:T(8,128)S(1)}, f32[2,40,512]{2,1,0:T(8,128)S(1)}, u32[]{:S(2)}, u32[]{:S(2)}) collective-permute-start(f32[2,40,512]{2,1,0:T(8,128)S(1)} %reduce_sum.9), channel_id=1, source_target_pairs={{0,1},{1,0},{2,3},{3,2},{4,5},{5,4},{6,7},{7,6},{8,9},{9,8},{10,11... | collective-permute-start | bytes 491528 | tf_op jit(solution)/shard_map/ppermute | solution.py:245
  30.7 6.7 %collective-permute-start.1 = (f32[4,40,512]{2,1,0:T(8,128)S(1)}, f32[4,40,512]{2,1,0:T(8,128)S(1)}, u32[]{:S(2)}, u32[]{:S(2)}) collective-permute-start(f32[4,40,512]{2,1,0:T(8,128)S(1)} %pad_maximum_fusion.s_ref), channel_id=1, source_target_pairs={{0,31},{1,2},{2,1},{3,4},{4,3},{5,6},{6,5},{7,8},{8,7},{9,10},{10,... | collective-permute-start | bytes 983048 | tf_op jit(solution)/shard_map/ppermute | solution.py:247
  37.7 7.5 %collective-permute-start.2 = (f32[2,40,512]{2,1,0:T(8,128)S(1)}, f32[2,40,512]{2,1,0:T(8,128)S(1)}, u32[]{:S(2)}, u32[]{:S(2)}) collective-permute-start(f32[2,40,512]{2,1,0:T(8,128)S(1)} %get-tuple-element.20.fz_ref), channel_id=1, source_target_pairs={{0,1},{1,0},{2,3},{3,2},{4,5},{5,4},{6,7},{7,6},{8,9},{9,8},{10,11... | collective-permute-start | bytes 491528 | tf_op jit(solution)/shard_map/ppermute | solution.py:250

commit v2 on v1

v2 whole, which is shorter than its diff:
```python
import functools
import math

import jax
import jax.numpy as jnp
from jax import lax
from jax.experimental import pallas as pl
from jax.experimental.pallas import tpu as pltpu
from jax.sharding import PartitionSpec as P

spacing = 0.25
denominator = 64.0
kappa = 0.804
mu = 0.2195149727645171
beta = 0.06672455060314922
gamma = (1.0 - math.log(2.0)) / math.pi**2
pw_a = 0.0310907
alpha1 = 0.2137
beta_over_gamma = beta / gamma
exch = 0.75 * (3.0 / math.pi) ** (1.0 / 3.0)
rs_unit = (3.0 / (4.0 * math.pi)) ** (1.0 / 3.0)
s_unit = 1.0 / (4.0 * (3.0 * math.pi**2) ** (2.0 / 3.0))
t_unit = math.pi / (16.0 * (3.0 * math.pi**2) ** (1.0 / 3.0))
q1 = 2.0 * pw_a * 7.5957 * rs_unit**0.5
q2 = 2.0 * pw_a * 3.5876 * rs_unit
q3 = 2.0 * pw_a * 1.6382 * rs_unit**1.5
q4 = 2.0 * pw_a * 0.49294 * rs_unit**2

third = 1.0 / (12.0 * spacing)
HALO = 4
VMEM_LIMIT = 40 * 1024 * 1024


def of_density(n, with_energy):
    w = jnp.exp(jnp.log(n) * (-1.0 / 6.0))
    q = w * (q1 + w * (q2 + w * (q3 + w * q4)))
    radius = rs_unit * (w * w)
    slope = 1.0 + alpha1 * radius
    log_term = jnp.log(1.0 + 1.0 / q)
    e_corr = (-2.0 * pw_a) * slope * log_term
    grown = jnp.exp(e_corr * (-1.0 / gamma))
    less = 1.0 / (grown - 1.0)
    factor = beta_over_gamma * less
    if not with_energy:
        return w, factor
    rq = w * (0.5 * q1 + w * (q2 + w * (1.5 * q3 + w * (2.0 * q4))))
    change = (2.0 * pw_a / 3.0) * (alpha1 * radius * log_term - slope * rq / (q * (q + 1.0)))
    return w, factor, e_corr + change, change * factor * (grown * less) * (1.0 / gamma)


def of_gradient(w, factor, g, energy=None):
    w2 = w * w
    w4 = w2 * w2
    w8 = w4 * w4
    s_sq = (s_unit * g) * (w8 * w8)
    t_sq = (t_unit * g) * (w8 * w4 * w2)
    u = factor * t_sq
    up = 1.0 + u
    d = up + u * u
    wide = d + beta_over_gamma * t_sq * up
    inv = 1.0 / (d * wide)
    h_t = beta * (1.0 + 2.0 * u) * inv
    inv_x = 1.0 / (1.0 + (mu / kappa) * s_sq)
    f_s = mu * inv_x * inv_x
    twice = (2.0 * w8) * (t_unit * h_t - (exch * s_unit) * f_s)
    if energy is None:
        return twice
    n, base, change = energy
    h = gamma * jnp.log(wide * wide * inv)
    h_a = -beta * (t_sq * t_sq) * u * (2.0 + u) * inv
    f_x = (1.0 + kappa) - kappa * inv_x
    e_n = base + h + change * h_a - (7.0 / 3.0) * t_sq * h_t
    e_n = e_n - (4.0 / 3.0 * exch) * (n * w4) * (f_x - 2.0 * s_sq * f_s)
    return twice, e_n


def roll(v, shift, axis):
    return pltpu.roll(v, shift % v.shape[axis], axis)


def d_along(v, axis):
    near = roll(v, -1, axis) - roll(v, 1, axis)
    far = roll(v, -2, axis) - roll(v, 2, axis)
    return (8.0 * third) * near - third * far


def d_z(p2, p1, m1, m2):
    return (8.0 * third) * (p1 - m1) - third * (p2 - m2)


def terms_kernel(occ_ref, states_ref, core_ref, out_ref, occ_held, held, core_held, sems):
    rows = held.shape[2]
    parts, _, wide, _ = out_ref.shape
    own = rows // parts
    pieces = sems.shape[0] - 4
    per = rows // pieces
    me = lax.axis_index("interval")
    flip = lax.rem(lax.axis_index("slab"), 2)
    first = pltpu.make_async_copy(occ_ref, occ_held, sems.at[pieces + 3])
    first.start()
    copies = []
    for k in range(pieces):
        at = pl.ds(k * per, per)
        copies.append(pltpu.make_async_copy(states_ref.at[:, :, at], held.at[:, :, at], sems.at[k]))
    low = pl.multiple_of(lax.rem(me * own + rows - 8, rows), 8)
    mid = pl.multiple_of(me * own, 8)
    top = pl.multiple_of(lax.rem(me * own + own, rows), 8)
    for k, (start, size, to) in enumerate(((low, 8, 0), (mid, own, 8), (top, 8, own + 8))):
        copies.append(
            pltpu.make_async_copy(
                core_ref.at[:, pl.ds(start, size)], core_held.at[:, pl.ds(to, size)], sems.at[pieces + k]
            )
        )
    for c in copies:
        c.start()
    first.wait()
    w0 = occ_held[0].astype(jnp.float32) * (1.0 / denominator)
    w1 = occ_held[1].astype(jnp.float32) * (1.0 / denominator)
    for k in range(pieces):
        copies[k].wait()
        for i in range(k * per // own, (k + 1) * per // own):
            for p in range(2):
                to = p ^ flip
                for r in range(0, own, 8):
                    a = held[0, p, pl.ds(i * own + r, 8)]
                    b = held[1, p, pl.ds(i * own + r, 8)]
                    t = w0 * a * a + w1 * b * b
                    out_ref[i, to, pl.ds(r + HALO, 8)] = t
                    if r == 0:
                        out_ref[(i - 1) % parts, to, pl.ds(own + HALO, HALO)] = t[:HALO]
                    if r == own - 8:
                        out_ref[(i + 1) % parts, to, pl.ds(0, HALO)] = t[8 - HALO:]
    for c in copies[pieces:]:
        c.wait()
    for p in range(2):
        to = p ^ flip
        out_ref[me, to] = out_ref[me, to] + core_held[p, pl.ds(8 - HALO, wide)]


def x_slopes(field, slopes):
    for p in range(2):
        for c in range(0, field.shape[2], 128):
            at = pl.ds(c, 128)
            slopes[p, :, at] = d_along(field[p, :, at], 0)


def own_kernel(s_ref, w_ref, a_ref, base_ref, change_ref, gx_ref, gy_ref):
    x_slopes(s_ref, gx_ref)
    for p in range(2):
        for r in range(0, s_ref.shape[1], 8):
            at = pl.ds(r, 8)
            n = s_ref[p, at]
            gy_ref[p, at] = d_along(n, 1)
            w_ref[p, at], a_ref[p, at], base_ref[p, at], change_ref[p, at] = of_density(n, True)


def mate_kernel(m_ref, w_ref, a_ref, flat_ref):
    x_slopes(m_ref, flat_ref)
    for p in range(2):
        for r in range(0, m_ref.shape[1], 8):
            at = pl.ds(r, 8)
            n = m_ref[p, at]
            gx, gy = flat_ref[p, at], d_along(n, 1)
            flat_ref[p, at] = gx * gx + gy * gy
            w_ref[p, at], a_ref[p, at] = of_density(n, False)


def ahead_kernel(s_ref, m_ref, far_ref, w_ref, a_ref, flat_ref, fz_ref):
    for r in range(0, s_ref.shape[1], 8):
        at = pl.ds(r, 8)
        s = (s_ref[0, at], s_ref[1, at], m_ref[1, at], m_ref[0, at], far_ref[0, at], far_ref[1, at])
        for p, gz in ((1, d_z(s[4], s[3], s[1], s[0])), (0, d_z(s[5], s[4], s[2], s[1]))):
            g = gz * gz + flat_ref[p, at]
            fz_ref[1 - p, at] = of_gradient(w_ref[p, at], a_ref[p, at], g) * gz


def last_kernel(
    s_ref, m_ref, n_ref, b_ref, w_ref, a_ref, base_ref, change_ref, gx_ref, gy_ref, fz_ref, out_ref, gxn, fx, part
):
    rows, cols = s_ref.shape[1:]
    own = rows - 2 * HALO
    flip = lax.rem(lax.axis_index("slab"), 2)
    x_slopes(n_ref, gxn)
    for r in range(0, rows, 8):
        at = pl.ds(r, 8)
        s = (s_ref[0, at], s_ref[1, at], m_ref[1, at], m_ref[0, at])
        n = (n_ref[0, at], n_ref[1, at], b_ref[1, at], b_ref[0, at])
        f = []
        for p, gz in ((0, d_z(s[1], s[0], n[1], n[2])), (1, d_z(s[0], n[0], n[2], n[3]))):
            gx, gy = gxn[p, at], d_along(n[p], 1)
            w, factor = of_density(n[p], False)
            f.append(of_gradient(w, factor, gz * gz + gx * gx + gy * gy) * gz)
        o = []
        for p, gz in ((0, d_z(s[2], s[1], n[0], n[1])), (1, d_z(s[3], s[2], s[0], n[0]))):
            gx, gy = gx_ref[p, at], gy_ref[p, at]
            g = gz * gz + gx * gx + gy * gy
            twice, e_n = of_gradient(
                w_ref[p, at], a_ref[p, at], g, (s[p], base_ref[p, at], change_ref[p, at])
            )
            fx[p, at] = twice * gx
            o.append(twice * gz)
            part[p, at] = e_n - d_along(twice * gy, 1)
        f2, f3 = fz_ref[0, at], fz_ref[1, at]
        part[0, at] = part[0, at] - d_z(f2, o[1], f[0], f[1])
        part[1, at] = part[1, at] - d_z(f3, f2, o[0], f[0])
    x_slopes(fx, gxn)
    for p in range(2):
        out_ref[p ^ flip] = part[p, pl.ds(HALO, own)] - gxn[p, pl.ds(HALO, own)]


def call(kernel, outs, *args, scratch=(), out_hbm=False, flops=0):
    f32 = jnp.float32
    return pl.pallas_call(
        kernel,
        out_shape=[jax.ShapeDtypeStruct(o, f32) if out_hbm else pltpu.VMEM(o, f32) for o in outs],
        in_specs=[pl.BlockSpec(memory_space=pltpu.VMEM)] * len(args),
        out_specs=[pl.BlockSpec(memory_space=pltpu.VMEM)] * len(outs),
        scratch_shapes=list(scratch),
        compiler_params=pltpu.CompilerParams(vmem_limit_bytes=VMEM_LIMIT),
        cost_estimate=pl.CostEstimate(
            flops=flops, bytes_accessed=4 * sum(math.prod(o) for o in outs), transcendentals=flops // 32
        ),
        name=kernel.__name__,
    )(*[pltpu.with_memory_space_constraint(a, pltpu.VMEM) for a in args])


def shards(states, occupations, core_density):
    f32 = jnp.float32
    parts = lax.axis_size("interval")
    slabs = lax.axis_size("slab")
    planes, rows, cols = core_density.shape
    own = rows // parts
    wide = own + 2 * HALO
    block = (planes, wide, cols)
    pieces = 4
    (terms,) = pl.pallas_call(
        terms_kernel,
        out_shape=[pltpu.VMEM((parts, *block), f32)],
        in_specs=[pl.BlockSpec(memory_space=pltpu.HBM)] * 3,
        out_specs=[pl.BlockSpec(memory_space=pltpu.VMEM)],
        scratch_shapes=[
            pltpu.SMEM(occupations.shape, jnp.int32),
            pltpu.VMEM(states.shape, f32),
            pltpu.VMEM((planes, own + 16, cols), f32),
            pltpu.SemaphoreType.DMA((pieces + 4,)),
        ],
        compiler_params=pltpu.CompilerParams(vmem_limit_bytes=VMEM_LIMIT),
        name="terms_kernel",
    )(*[pltpu.with_memory_space_constraint(a, pltpu.HBM) for a in (occupations, states, core_density)])
    density = jnp.sum(lax.all_to_all(terms, "interval", 0, 0), axis=0)
    chips = slabs // 2
    beside = lambda q, odd: (q + (1 if q % 2 == odd else -1)) % chips
    odd_pairs = [(s, 2 * beside(s // 2, 1) + s % 2) for s in range(slabs)]
    even_pairs = [(s, 2 * beside(s // 2, 0) + s % 2) for s in range(slabs)]
    mates = [(s, s ^ 1) for s in range(slabs)]
    from_even = lax.ppermute(density, "slab", even_pairs)
    from_odd = lax.ppermute(density, "slab", odd_pairs)
    mate = lax.ppermute(density, "slab", mates)
    w, factor, base, change, gx, gy = call(own_kernel, [block] * 6, density, flops=100_000_000)
    w_m, factor_m, flat_m = call(mate_kernel, [block] * 3, mate, flops=100_000_000)
    from_odd, from_even, w, w_m = lax.optimization_barrier((from_odd, from_even, w, w_m))
    at = lax.axis_index("slab")
    odd_ahead = lax.rem(at // 2 + at, 2) == 1
    ahead = jnp.where(odd_ahead, from_odd, from_even)
    behind = jnp.where(odd_ahead, from_even, from_odd)
    near = lax.ppermute(ahead, "slab", mates)
    (fz,) = call(ahead_kernel, [block], density, mate, ahead, w_m, factor_m, flat_m, flops=50_000_000)
    (out,) = call(
        last_kernel, [(planes, own, cols)],
        density, mate, near, behind, w, factor, base, change, gx, gy, fz,
        scratch=[pltpu.VMEM(block, f32)] * 3, out_hbm=True,
    )
    return out


def solution(mesh):
    return jax.shard_map(
        shards,
        mesh=mesh,
        in_specs=(P("interval", "slab", None, None), P("interval"), P("slab", None, None)),
        out_specs=P("slab", "interval", None),
        check_vma=False,
    )
```

time: 46.1 us -> 44.3 us (0.961)
  local copies, waits for them, and re-layouts: 3.48 us -> 0 us
  Pallas kernels: 3.5 us -> 4.39 us
  starting transfers between devices: 10.5 us -> 11.2 us
    unnamed x6 -> x0, local copies, waits for them, and re-layouts: 3.47 us -> none
    ppermute x2 -> x3, waiting for transfers between devices: 4.37 us -> 5.5 us  [the longest x1 3.73 us: shards(): from_odd = lax.ppermute(density, 'slab', odd_pairs)]
    ppermute x1, waiting for transfers between devices: 1.03 us -> 0.01 us  [shards(): mate = lax.ppermute(density, 'slab', mates)]
    pallas_call x5, Pallas kernels: 3.5 us -> 4.39 us  [the longest x4 2.72 us: call(): pl.pallas_call(kernel, out_shape=[jax.ShapeDtypeStruct(o, f32) if out_hbm...]
    ppermute x2 -> x3, starting transfers between devices: 8.48 us -> 9.21 us  [the longest x1 7.93 us: shards(): from_odd = lax.ppermute(density, 'slab', odd_pairs)]
  transfers between devices with their start and end apart: 3 -> 4, of which waited for: 2 -> 3; matrix products, arithmetic and copies ran while one was open for 0% -> 0% of each run, Pallas kernels for 3% -> 2%
where the time goes in v2:
time: 44.3 us; the launch traced here: 44.1 us
  blocking collectives  22.8 us (51%)
  starting transfers between devices  11.2 us (25%)
  waiting for transfers between devices  5.5 us (12%)
  Pallas kernels  4.39 us (10%)
    all_to_all x1, blocking collectives, shards(): density = jnp.sum(lax.all_to_all(terms, 'interval', 0, 0), axis=0)  22.8 us
    ppermute x1, starting transfers between devices, shards(): from_odd = lax.ppermute(density, 'slab', odd_pairs)  7.93 us
    ppermute x1, waiting for transfers between devices, shards(): from_odd = lax.ppermute(density, 'slab', odd_pairs)  3.73 us
    pallas_call x4, Pallas kernels, call(): pl.pallas_call(kernel, out_shape=[jax.ShapeDtypeStruct(o, f32) if out_hbm...  2.72 us
    ppermute x1, starting transfers between devices, shards(): mate = lax.ppermute(density, 'slab', mates)  2.03 us
    pallas_call x1, Pallas kernels, shards(): pl.pallas_call(terms_kernel, out_shape=[pltpu.VMEM((parts, *block), f32)]...  1.67 us
    ppermute x1, starting transfers between devices, shards(): near = lax.ppermute(ahead, 'slab', mates)  1.28 us
    ppermute x1, waiting for transfers between devices, shards(): from_even = lax.ppermute(density, 'slab', even_pairs)  0.97 us
  transfers between devices with their start and end apart: 4, of which 3 were waited for; matrix products, arithmetic and copies ran while one was open for 0% of the time, Pallas kernels for 2%

profile of v2, /device:TPU:1, one launch (start us, length us, event | category | flops | bytes accessed | tf_op | source)
XLA Modules:
  0.0 44.1 jit_solution(459546282684461918)
XLA Ops:
  0.0 1.7 %terms_kernel.1 = f32[8,2,40,512]{3,2,1,0:T(8,128)S(1)} custom-call(s32[2]{0:T(128)} %occ_ref.1, f32[2,2,256,512]{3,2,1,0:T(8,128)} %states_ref.1, f32[2,256,512]{2,1,0:T(8,128)} %core_ref.1), custom_call_target="tpu_custom_call" | custom-call | tf_op jit(solution)/shard_map/terms_kernel/pallas_call | solution.py:236
  1.7 22.8 %all_to_all.5 = f32[8,2,40,512]{3,2,1,0:T(8,128)S(1)} all-to-all(f32[8,2,40,512]{3,2,1,0:T(8,128)S(1)} %terms_kernel.1), channel_id=1, replica_groups=mesh['interval'=8,'slab'=32] {'interval'}, dimensions={0} | all-to-all | bytes 2621440 | tf_op jit(solution)/shard_map/all_to_all | solution.py:250
  24.5 0.1 reduce_sum.9.s_ref
  24.6 2.0 %collective-permute-start = (f32[2,40,512]{2,1,0:T(8,128)S(1)}, f32[2,40,512]{2,1,0:T(8,128)S(1)}, u32[]{:S(2)}, u32[]{:S(2)}) collective-permute-start(f32[2,40,512]{2,1,0:T(8,128)S(1)} %reduce_sum.9.s_ref), channel_id=1, source_target_pairs={{0,1},{1,0},{2,3},{3,2},{4,5},{5,4},{6,7},{7,6},{8,9},{9,8},{10,11... | collective-permute-start | bytes 491528 | tf_op jit(solution)/shard_map/ppermute | solution.py:258
  26.6 7.9 %collective-permute-start.1 = (f32[2,40,512]{2,1,0:T(8,128)S(1)}, f32[2,40,512]{2,1,0:T(8,128)S(1)}, u32[]{:S(2)}, u32[]{:S(2)}) collective-permute-start(f32[2,40,512]{2,1,0:T(8,128)S(1)} %reduce_sum.9.s_ref), channel_id=1, source_target_pairs={{0,30},{1,31},{2,4},{3,5},{4,2},{5,3},{6,8},{7,9},{8,6},{9,7},{10,... | collective-permute-start | bytes 491528 | tf_op jit(solution)/shard_map/ppermute | solution.py:257
  34.6 0.0 collective-permute-start.2
  34.6 0.4 own_kernel.1
  35.0 0.0 collective-permute-done.m_ref
  35.0 0.3 mate_kernel.1
  35.3 3.7 %collective-permute-done.1 = f32[2,40,512]{2,1,0:T(8,128)S(1)} collective-permute-done((f32[2,40,512]{2,1,0:T(8,128)S(1)}, f32[2,40,512]{2,1,0:T(8,128)S(1)}, u32[]{:S(2)}, u32[]{:S(2)}) %collective-permute-start.1) | collective-permute-done | bytes 163872 | tf_op jit(solution)/shard_map/ppermute | solution.py:257
  39.0 1.0 %collective-permute-done.2 = f32[2,40,512]{2,1,0:T(8,128)S(1)} collective-permute-done((f32[2,40,512]{2,1,0:T(8,128)S(1)}, f32[2,40,512]{2,1,0:T(8,128)S(1)}, u32[]{:S(2)}, u32[]{:S(2)}) %collective-permute-start.2) | collective-permute-done | bytes 163872 | tf_op jit(solution)/shard_map/ppermute | solution.py:256
  40.0 1.3 %collective-permute-start.3 = (f32[2,40,512]{2,1,0:T(8,128)S(1)}, f32[2,40,512]{2,1,0:T(8,128)S(1)}, u32[]{:S(2)}, u32[]{:S(2)}) collective-permute-start(f32[2,40,512]{2,1,0:T(8,128)S(1)} %get-tuple-element.32.far_ref), channel_id=1, source_target_pairs={{0,1},{1,0},{2,3},{3,2},{4,5},{5,4},{6,7},{7,6},{8,9},{9,8},{10,11... | collective-permute-start | bytes 491528 | tf_op jit(solution)/shard_map/ppermute | solution.py:266
  41.3 0.2 ahead_kernel.1.fz_ref
  41.5 0.8 %collective-permute-done.3.n_ref = f32[2,40,512]{2,1,0:T(8,128)S(1)} collective-permute-done((f32[2,40,512]{2,1,0:T(8,128)S(1)}, f32[2,40,512]{2,1,0:T(8,128)S(1)}, u32[]{:S(2)}, u32[]{:S(2)}) %collective-permute-start.3) | collective-permute-done | bytes 163872 | tf_op jit(solution)/shard_map/ppermute | solution.py:266
  42.3 1.8 %last_kernel.1 = f32[2,32,512]{2,1,0:T(8,128)} custom-call(f32[2,40,512]{2,1,0:T(8,128)S(1)} %reduce_sum.9.s_ref, f32[2,40,512]{2,1,0:T(8,128)S(1)} %collective-permute-done.m_ref, f32[2,40,512]{2,1,0:T(8,128)S(1)} %collective-permute-done.3.n_ref, f32[2,40,512]{2,1,0:T(8,128)S(1)} %get-tuple-element.31.b_ref, f32[2,40,512]{2,1,0:T(8,128)S(1)} %get-tuple-element.22.w_ref, ...), custom_call_target="tpu_custom_call" | custom-call | bytes 131072 | tf_op jit(solution)/shard_map/last_kernel/pallas_call | solution.py:213
  (1 shorter events, 0.0 us)
Async XLA Ops:
  24.6 10.4 %collective-permute-start = (f32[2,40,512]{2,1,0:T(8,128)S(1)}, f32[2,40,512]{2,1,0:T(8,128)S(1)}, u32[]{:S(2)}, u32[]{:S(2)}) collective-permute-start(f32[2,40,512]{2,1,0:T(8,128)S(1)} %reduce_sum.9.s_ref), channel_id=1, source_target_pairs={{0,1},{1,0},{2,3},{3,2},{4,5},{5,4},{6,7},{7,6},{8,9},{9,8},{10,11... | collective-permute-start | bytes 491528 | tf_op jit(solution)/shard_map/ppermute | solution.py:258
  26.6 12.4 %collective-permute-start.1 = (f32[2,40,512]{2,1,0:T(8,128)S(1)}, f32[2,40,512]{2,1,0:T(8,128)S(1)}, u32[]{:S(2)}, u32[]{:S(2)}) collective-permute-start(f32[2,40,512]{2,1,0:T(8,128)S(1)} %reduce_sum.9.s_ref), channel_id=1, source_target_pairs={{0,30},{1,31},{2,4},{3,5},{4,2},{5,3},{6,8},{7,9},{8,6},{9,7},{10,... | collective-permute-start | bytes 491528 | tf_op jit(solution)/shard_map/ppermute | solution.py:257
  34.6 5.4 %collective-permute-start.2 = (f32[2,40,512]{2,1,0:T(8,128)S(1)}, f32[2,40,512]{2,1,0:T(8,128)S(1)}, u32[]{:S(2)}, u32[]{:S(2)}) collective-permute-start(f32[2,40,512]{2,1,0:T(8,128)S(1)} %reduce_sum.9.s_ref), channel_id=1, source_target_pairs={{0,2},{1,3},{2,0},{3,1},{4,6},{5,7},{6,4},{7,5},{8,10},{9,11},{10,... | collective-permute-start | bytes 491528 | tf_op jit(solution)/shard_map/ppermute | solution.py:256
  40.0 2.3 %collective-permute-start.3 = (f32[2,40,512]{2,1,0:T(8,128)S(1)}, f32[2,40,512]{2,1,0:T(8,128)S(1)}, u32[]{:S(2)}, u32[]{:S(2)}) collective-permute-start(f32[2,40,512]{2,1,0:T(8,128)S(1)} %get-tuple-element.32.far_ref), channel_id=1, source_target_pairs={{0,1},{1,0},{2,3},{3,2},{4,5},{5,4},{6,7},{7,6},{8,9},{9,8},{10,11... | collective-permute-start | bytes 491528 | tf_op jit(solution)/shard_map/ppermute | solution.py:266

commit v3 on v2

--- a/solution.py
+++ b/solution.py
@@ -90,7 +90,7 @@
 
 def terms_kernel(occ_ref, states_ref, core_ref, out_ref, occ_held, held, core_held, sems):
     rows = held.shape[2]
-    parts, _, wide, _ = out_ref.shape
+    parts = out_ref.shape[0]
     own = rows // parts
     pieces = sems.shape[0] - 4
     per = rows // pieces
@@ -105,7 +105,7 @@
     low = pl.multiple_of(lax.rem(me * own + rows - 8, rows), 8)
     mid = pl.multiple_of(me * own, 8)
     top = pl.multiple_of(lax.rem(me * own + own, rows), 8)
-    for k, (start, size, to) in enumerate(((low, 8, 0), (mid, own, 8), (top, 8, own + 8))):
+    for k, (start, size, to) in enumerate(((mid, own, 0), (top, 8, own), (low, 8, own + 8))):
         copies.append(
             pltpu.make_async_copy(
                 core_ref.at[:, pl.ds(start, size)], core_held.at[:, pl.ds(to, size)], sems.at[pieces + k]
@@ -125,16 +125,18 @@
                     a = held[0, p, pl.ds(i * own + r, 8)]
                     b = held[1, p, pl.ds(i * own + r, 8)]
                     t = w0 * a * a + w1 * b * b
-                    out_ref[i, to, pl.ds(r + HALO, 8)] = t
+                    out_ref[i, to, pl.ds(r, 8)] = t
                     if r == 0:
-                        out_ref[(i - 1) % parts, to, pl.ds(own + HALO, HALO)] = t[:HALO]
+                        out_ref[(i - 1) % parts, to, pl.ds(own, HALO)] = t[:HALO]
                     if r == own - 8:
-                        out_ref[(i + 1) % parts, to, pl.ds(0, HALO)] = t[8 - HALO:]
+                        out_ref[(i + 1) % parts, to, pl.ds(own + HALO, HALO)] = t[HALO:]
     for c in copies[pieces:]:
         c.wait()
     for p in range(2):
         to = p ^ flip
-        out_ref[me, to] = out_ref[me, to] + core_held[p, pl.ds(8 - HALO, wide)]
+        for to_row, size, row in ((0, own, 0), (own, HALO, own), (own + HALO, HALO, own + 8 + HALO)):
+            at = pl.ds(to_row, size)
+            out_ref[me, to, at] = out_ref[me, to, at] + core_held[p, pl.ds(row, size)]
 
 
 def x_slopes(field, slopes):
@@ -151,61 +153,68 @@
             at = pl.ds(r, 8)
             n = s_ref[p, at]
             gy_ref[p, at] = d_along(n, 1)
-            w_ref[p, at], a_ref[p, at], base_ref[p, at], change_ref[p, at] = of_density(n, True)
-
-
-def mate_kernel(m_ref, w_ref, a_ref, flat_ref):
-    x_slopes(m_ref, flat_ref)
-    for p in range(2):
-        for r in range(0, m_ref.shape[1], 8):
-            at = pl.ds(r, 8)
-            n = m_ref[p, at]
-            gx, gy = flat_ref[p, at], d_along(n, 1)
-            flat_ref[p, at] = gx * gx + gy * gy
-            w_ref[p, at], a_ref[p, at] = of_density(n, False)
-
-
-def ahead_kernel(s_ref, m_ref, far_ref, w_ref, a_ref, flat_ref, fz_ref):
-    for r in range(0, s_ref.shape[1], 8):
-        at = pl.ds(r, 8)
-        s = (s_ref[0, at], s_ref[1, at], m_ref[1, at], m_ref[0, at], far_ref[0, at], far_ref[1, at])
-        for p, gz in ((1, d_z(s[4], s[3], s[1], s[0])), (0, d_z(s[5], s[4], s[2], s[1]))):
-            g = gz * gz + flat_ref[p, at]
-            fz_ref[1 - p, at] = of_gradient(w_ref[p, at], a_ref[p, at], g) * gz
-
-
-def last_kernel(
-    s_ref, m_ref, n_ref, b_ref, w_ref, a_ref, base_ref, change_ref, gx_ref, gy_ref, fz_ref, out_ref, gxn, fx, part
-):
-    rows, cols = s_ref.shape[1:]
+            if r < s_ref.shape[1] - 2 * HALO:
+                w_ref[p, at], a_ref[p, at], base_ref[p, at], change_ref[p, at] = of_density(n, True)
+            else:
+                w_ref[p, at], a_ref[p, at] = of_density(n, False)
+
+
+def flux_kernel(s_ref, m_ref, n_ref, w_ref, a_ref, gx_ref, gy_ref, fz_ref, g_ref, twice_ref):
+    rows = s_ref.shape[1]
     own = rows - 2 * HALO
-    flip = lax.rem(lax.axis_index("slab"), 2)
-    x_slopes(n_ref, gxn)
     for r in range(0, rows, 8):
         at = pl.ds(r, 8)
         s = (s_ref[0, at], s_ref[1, at], m_ref[1, at], m_ref[0, at])
+        n = (n_ref[0, at], n_ref[1, at])
+        for p, gz in ((0, d_z(s[2], s[1], n[0], n[1])), (1, d_z(s[3], s[2], s[0], n[0]))):
+            gx, gy = gx_ref[p, at], gy_ref[p, at]
+            g = gz * gz + gx * gx + gy * gy
+            twice = of_gradient(w_ref[p, at], a_ref[p, at], g)
+            g_ref[p, at] = g
+            twice_ref[p, at] = twice
+            if r < own:
+                fz_ref[p, at] = twice * gz
+
+
+def flat_kernel(
+    s_ref, n_ref, w_ref, a_ref, base_ref, change_ref, gx_ref, gy_ref, g_ref, twice_ref,
+    part_ref, wn_ref, an_ref, flat_ref, slopes, fx
+):
+    rows = s_ref.shape[1]
+    own = rows - 2 * HALO
+    for p in range(2):
+        for r in range(0, rows, 8):
+            at = pl.ds(r, 8)
+            fx[p, at] = twice_ref[p, at] * gx_ref[p, at]
+    x_slopes(fx, slopes)
+    x_slopes(n_ref, fx)
+    for r in range(0, own, 8):
+        at = pl.ds(r, 8)
+        for p in range(2):
+            _, e_n = of_gradient(
+                w_ref[p, at], a_ref[p, at], g_ref[p, at], (s_ref[p, at], base_ref[p, at], change_ref[p, at])
+            )
+            part_ref[p, at] = e_n - slopes[p, at] - d_along(twice_ref[p, at] * gy_ref[p, at], 1)
+            n = n_ref[p, at]
+            gx, gy = fx[p, at], d_along(n, 1)
+            flat_ref[p, at] = gx * gx + gy * gy
+            wn_ref[p, at], an_ref[p, at] = of_density(n, False)
+
+
+def last_kernel(s_ref, n_ref, b_ref, part_ref, wn_ref, an_ref, flat_ref, fz_ref, fm_ref, out_ref):
+    own = part_ref.shape[1]
+    flip = lax.rem(lax.axis_index("slab"), 2)
+    for r in range(0, own, 8):
+        at = pl.ds(r, 8)
+        s = (s_ref[0, at], s_ref[1, at])
         n = (n_ref[0, at], n_ref[1, at], b_ref[1, at], b_ref[0, at])
         f = []
         for p, gz in ((0, d_z(s[1], s[0], n[1], n[2])), (1, d_z(s[0], n[0], n[2], n[3]))):
-            gx, gy = gxn[p, at], d_along(n[p], 1)
-            w, factor = of_density(n[p], False)
-            f.append(of_gradient(w, factor, gz * gz + gx * gx + gy * gy) * gz)
-        o = []
-        for p, gz in ((0, d_z(s[2], s[1], n[0], n[1])), (1, d_z(s[3], s[2], s[0], n[0]))):
-            gx, gy = gx_ref[p, at], gy_ref[p, at]
-            g = gz * gz + gx * gx + gy * gy
-            twice, e_n = of_gradient(
-                w_ref[p, at], a_ref[p, at], g, (s[p], base_ref[p, at], change_ref[p, at])
-            )
-            fx[p, at] = twice * gx
-            o.append(twice * gz)
-            part[p, at] = e_n - d_along(twice * gy, 1)
-        f2, f3 = fz_ref[0, at], fz_ref[1, at]
-        part[0, at] = part[0, at] - d_z(f2, o[1], f[0], f[1])
-        part[1, at] = part[1, at] - d_z(f3, f2, o[0], f[0])
-    x_slopes(fx, gxn)
-    for p in range(2):
-        out_ref[p ^ flip] = part[p, pl.ds(HALO, own)] - gxn[p, pl.ds(HALO, own)]
+            f.append(of_gradient(wn_ref[p, at], an_ref[p, at], gz * gz + flat_ref[p, at]) * gz)
+        f0, f1 = fz_ref[0, at], fz_ref[1, at]
+        f2, f3 = -fm_ref[1, at], -fm_ref[0, at]
+        out_ref[flip, at] = part_ref[0, at] - d_z(f2, f1, f[0], f[1])
+        out_ref[1 - flip, at] = part_ref[1, at] - d_z(f3, f2, f0, f[0])
 
 
 def call(kernel, outs, *args, scratch=(), out_hbm=False, flops=0):
@@ -250,25 +259,31 @@
     density = jnp.sum(lax.all_to_all(terms, "interval", 0, 0), axis=0)
     chips = slabs // 2
     beside = lambda q, odd: (q + (1 if q % 2 == odd else -1)) % chips
-    odd_pairs = [(s, 2 * beside(s // 2, 1) + s % 2) for s in range(slabs)]
-    even_pairs = [(s, 2 * beside(s // 2, 0) + s % 2) for s in range(slabs)]
+    odd_pairs = [(s, 2 * beside(s // 2, 1) + 1 - s % 2) for s in range(slabs)]
+    even_pairs = [(s, 2 * beside(s // 2, 0) + 1 - s % 2) for s in range(slabs)]
     mates = [(s, s ^ 1) for s in range(slabs)]
     from_even = lax.ppermute(density, "slab", even_pairs)
     from_odd = lax.ppermute(density, "slab", odd_pairs)
     mate = lax.ppermute(density, "slab", mates)
     w, factor, base, change, gx, gy = call(own_kernel, [block] * 6, density, flops=100_000_000)
-    w_m, factor_m, flat_m = call(mate_kernel, [block] * 3, mate, flops=100_000_000)
-    from_odd, from_even, w, w_m = lax.optimization_barrier((from_odd, from_even, w, w_m))
+    from_odd, from_even, w = lax.optimization_barrier((from_odd, from_even, w))
     at = lax.axis_index("slab")
-    odd_ahead = lax.rem(at // 2 + at, 2) == 1
-    ahead = jnp.where(odd_ahead, from_odd, from_even)
-    behind = jnp.where(odd_ahead, from_even, from_odd)
-    near = lax.ppermute(ahead, "slab", mates)
-    (fz,) = call(ahead_kernel, [block], density, mate, ahead, w_m, factor_m, flat_m, flops=50_000_000)
+    odd_near = lax.rem(at // 2 + at, 2) == 0
+    near = jnp.where(odd_near, from_odd, from_even)
+    other = jnp.where(odd_near, from_even, from_odd)[:, :own]
+    far = lax.ppermute(other, "slab", mates)
+    kept = (planes, own, cols)
+    fz, g, twice = call(
+        flux_kernel, [kept, block, block], density, mate, near, w, factor, gx, gy, flops=50_000_000
+    )
+    fz_mate = lax.ppermute(fz, "slab", mates)
+    part, w_n, factor_n, flat_n = call(
+        flat_kernel, [kept] * 4, density, near, w, factor, base, change, gx, gy, g, twice,
+        scratch=[pltpu.VMEM(block, f32)] * 2, flops=100_000_000,
+    )
+    far, fz_mate, part = lax.optimization_barrier((far, fz_mate, part))
     (out,) = call(
-        last_kernel, [(planes, own, cols)],
-        density, mate, near, behind, w, factor, base, change, gx, gy, fz,
-        scratch=[pltpu.VMEM(block, f32)] * 3, out_hbm=True,
+        last_kernel, [kept], density, near, far, part, w_n, factor_n, flat_n, fz, fz_mate, out_hbm=True
     )
     return out
 

time: 44.3 us -> 42.2 us (0.953)
  waiting for transfers between devices: 5.5 us -> 4.73 us
  starting transfers between devices: 11.2 us -> 10.5 us
  Pallas kernels: 4.39 us -> 3.76 us
    ppermute x1, starting transfers between devices: 2.03 us -> 0.01 us  [shards(): mate = lax.ppermute(density, 'slab', mates)]
    ppermute x1, starting transfers between devices: 7.93 us -> 9.83 us  [shards(): from_odd = lax.ppermute(density, 'slab', odd_pairs)]
    ppermute x1, waiting for transfers between devices: 3.73 us -> 2.62 us  [shards(): from_odd = lax.ppermute(density, 'slab', odd_pairs)]
    ppermute x1, waiting for transfers between devices: 0.97 us -> 1.74 us  [shards(): from_even = lax.ppermute(density, 'slab', even_pairs)]
    pallas_call x4, Pallas kernels: 2.72 us -> 2.1 us  [call(): pl.pallas_call(kernel, out_shape=[jax.ShapeDtypeStruct(o, f32) if out_hbm...]
    ppermute x1 -> x2, starting transfers between devices: 1.28 us -> 0.67 us  [the longest x1 0.58 us: shards(): fz_mate = lax.ppermute(fz, 'slab', mates)]
  transfers between devices with their start and end apart: 4 -> 5, of which waited for: 3 -> 3; matrix products, arithmetic and copies ran while one was open for 0% -> 0% of each run, Pallas kernels for 2% -> 3%
where the time goes in v3:
time: 42.2 us; the launch traced here: 42 us
  blocking collectives  22.8 us (54%)
  starting transfers between devices  10.5 us (25%)
  waiting for transfers between devices  4.73 us (11%)
  Pallas kernels  3.76 us (9%)
    all_to_all x1, blocking collectives, shards(): density = jnp.sum(lax.all_to_all(terms, 'interval', 0, 0), axis=0)  22.8 us
    ppermute x1, starting transfers between devices, shards(): from_odd = lax.ppermute(density, 'slab', odd_pairs)  9.83 us
    ppermute x1, waiting for transfers between devices, shards(): from_odd = lax.ppermute(density, 'slab', odd_pairs)  2.62 us
    pallas_call x4, Pallas kernels, call(): pl.pallas_call(kernel, out_shape=[jax.ShapeDtypeStruct(o, f32) if out_hbm...  2.1 us
    ppermute x1, waiting for transfers between devices, shards(): from_even = lax.ppermute(density, 'slab', even_pairs)  1.74 us
    pallas_call x1, Pallas kernels, shards(): pl.pallas_call(terms_kernel, out_shape=[pltpu.VMEM((parts, *block), f32)]...  1.66 us
  transfers between devices with their start and end apart: 5, of which 3 were waited for; matrix products, arithmetic and copies ran while one was open for 0% of the time, Pallas kernels for 3%

profile of v3, /device:TPU:1, one launch (start us, length us, event | category | flops | bytes accessed | tf_op | source)
XLA Modules:
  0.0 42.0 jit_solution(14684050217745129044)
XLA Ops:
  0.0 1.7 %terms_kernel.1 = f32[8,2,40,512]{3,2,1,0:T(8,128)S(1)} custom-call(s32[2]{0:T(128)} %occ_ref.1, f32[2,2,256,512]{3,2,1,0:T(8,128)} %states_ref.1, f32[2,256,512]{2,1,0:T(8,128)} %core_ref.1), custom_call_target="tpu_custom_call" | custom-call | tf_op jit(solution)/shard_map/terms_kernel/pallas_call | solution.py:245
  1.7 22.8 %all_to_all.5 = f32[8,2,40,512]{3,2,1,0:T(8,128)S(1)} all-to-all(f32[8,2,40,512]{3,2,1,0:T(8,128)S(1)} %terms_kernel.1), channel_id=1, replica_groups=mesh['interval'=8,'slab'=32] {'interval'}, dimensions={0} | all-to-all | bytes 2621440 | tf_op jit(solution)/shard_map/all_to_all | solution.py:259
  24.5 0.1 reduce_sum.9.s_ref
  24.6 9.8 %collective-permute-start = (f32[2,40,512]{2,1,0:T(8,128)S(1)}, f32[2,40,512]{2,1,0:T(8,128)S(1)}, u32[]{:S(2)}, u32[]{:S(2)}) collective-permute-start(f32[2,40,512]{2,1,0:T(8,128)S(1)} %reduce_sum.9.s_ref), channel_id=1, source_target_pairs={{0,31},{1,30},{2,5},{3,4},{4,3},{5,2},{6,9},{7,8},{8,7},{9,6},{10,... | collective-permute-start | bytes 491528 | tf_op jit(solution)/shard_map/ppermute | solution.py:266
  34.4 0.0 collective-permute-start.1
  34.4 0.0 collective-permute-start.3
  34.4 0.4 own_kernel.1
  34.8 2.6 %collective-permute-done = f32[2,40,512]{2,1,0:T(8,128)S(1)} collective-permute-done((f32[2,40,512]{2,1,0:T(8,128)S(1)}, f32[2,40,512]{2,1,0:T(8,128)S(1)}, u32[]{:S(2)}, u32[]{:S(2)}) %collective-permute-start) | collective-permute-done | bytes 163872 | tf_op jit(solution)/shard_map/ppermute | solution.py:266
  37.4 1.7 %collective-permute-done.1 = f32[2,40,512]{2,1,0:T(8,128)S(1)} collective-permute-done((f32[2,40,512]{2,1,0:T(8,128)S(1)}, f32[2,40,512]{2,1,0:T(8,128)S(1)}, u32[]{:S(2)}, u32[]{:S(2)}) %collective-permute-start.1) | collective-permute-done | bytes 163872 | tf_op jit(solution)/shard_map/ppermute | solution.py:265
  39.2 0.1 collective-permute-start.2
  39.3 0.0 collective-permute-done.3.m_ref
  39.3 0.2 flux_kernel.1
  39.6 0.6 %collective-permute-start.4 = (f32[2,32,512]{2,1,0:T(8,128)S(1)}, f32[2,32,512]{2,1,0:T(8,128)S(1)}, u32[]{:S(2)}, u32[]{:S(2)}) collective-permute-start(f32[2,32,512]{2,1,0:T(8,128)S(1)} %get-tuple-element.31.fz_ref), channel_id=1, source_target_pairs={{0,1},{1,0},{2,3},{3,2},{4,5},{5,4},{6,7},{7,6},{8,9},{9,8},{10,11... | collective-permute-start | bytes 393224 | tf_op jit(solution)/shard_map/ppermute | solution.py:279
  40.2 0.6 %flat_kernel.1 = (f32[2,32,512]{2,1,0:T(8,128)S(1)}, f32[2,32,512]{2,1,0:T(8,128)S(1)}, f32[2,32,512]{2,1,0:T(8,128)S(1)}, f32[2,32,512]{2,1,0:T(8,128)S(1)}) custom-call(f32[2,40,512]{2,1,0:T(8,128)S(1)} %reduce_sum.9.s_ref, f32[2,40,512]{2,1,0:T(8,128)S(1)} %broadcast_select_fusion.n_ref, f32[2,40,512]{2,1,0:T(8,128)S(1)} %get-tuple-element.27.w_ref, ...), custom_call_target="tpu_custom_call" | custom-call | flops 100000000 | bytes 524288 | tf_op jit(solution)/shard_map/flat_kernel/pallas_call | solution.py:222
  40.8 0.0 collective-permute-done.2.b_ref
  40.8 0.4 collective-permute-done.4.fm_ref
  41.2 0.9 %last_kernel.1 = f32[2,32,512]{2,1,0:T(8,128)} custom-call(f32[2,40,512]{2,1,0:T(8,128)S(1)} %reduce_sum.9.s_ref, f32[2,40,512]{2,1,0:T(8,128)S(1)} %broadcast_select_fusion.n_ref, f32[2,32,512]{2,1,0:T(8,128)S(1)} %collective-permute-done.2.b_ref, f32[2,32,512]{2,1,0:T(8,128)S(1)} %get-tuple-element.38.part_ref, ...), custom_call_target="tpu_custom_call" | custom-call | bytes 131072 | tf_op jit(solution)/shard_map/last_kernel/pallas_call | solution.py:222
  (2 shorter events, 0.0 us)
Async XLA Ops:
  24.6 12.8 %collective-permute-start = (f32[2,40,512]{2,1,0:T(8,128)S(1)}, f32[2,40,512]{2,1,0:T(8,128)S(1)}, u32[]{:S(2)}, u32[]{:S(2)}) collective-permute-start(f32[2,40,512]{2,1,0:T(8,128)S(1)} %reduce_sum.9.s_ref), channel_id=1, source_target_pairs={{0,31},{1,30},{2,5},{3,4},{4,3},{5,2},{6,9},{7,8},{8,7},{9,6},{10,... | collective-permute-start | bytes 491528 | tf_op jit(solution)/shard_map/ppermute | solution.py:266
  34.4 4.7 %collective-permute-start.1 = (f32[2,40,512]{2,1,0:T(8,128)S(1)}, f32[2,40,512]{2,1,0:T(8,128)S(1)}, u32[]{:S(2)}, u32[]{:S(2)}) collective-permute-start(f32[2,40,512]{2,1,0:T(8,128)S(1)} %reduce_sum.9.s_ref), channel_id=1, source_target_pairs={{0,3},{1,2},{2,1},{3,0},{4,7},{5,6},{6,5},{7,4},{8,11},{9,10},{10,... | collective-permute-start | bytes 491528 | tf_op jit(solution)/shard_map/ppermute | solution.py:265
  34.4 4.9 %collective-permute-start.3 = (f32[2,40,512]{2,1,0:T(8,128)S(1)}, f32[2,40,512]{2,1,0:T(8,128)S(1)}, u32[]{:S(2)}, u32[]{:S(2)}) collective-permute-start(f32[2,40,512]{2,1,0:T(8,128)S(1)} %reduce_sum.9.s_ref), channel_id=1, source_target_pairs={{0,1},{1,0},{2,3},{3,2},{4,5},{5,4},{6,7},{7,6},{8,9},{9,8},{10,11... | collective-permute-start | bytes 491528 | tf_op jit(solution)/shard_map/ppermute | solution.py:267
  39.2 1.6 %collective-permute-start.2 = (f32[2,32,512]{2,1,0:T(8,128)S(1)}, f32[2,32,512]{2,1,0:T(8,128)S(1)}, u32[]{:S(2)}, u32[]{:S(2)}) collective-permute-start(f32[2,32,512]{2,1,0:T(8,128)S(1)} %slice_select_fusion), channel_id=1, source_target_pairs={{0,1},{1,0},{2,3},{3,2},{4,5},{5,4},{6,7},{7,6},{8,9},{9,8},{10,11... | collective-permute-start | bytes 393224 | tf_op jit(solution)/shard_map/ppermute | solution.py:274
  39.6 1.6 %collective-permute-start.4 = (f32[2,32,512]{2,1,0:T(8,128)S(1)}, f32[2,32,512]{2,1,0:T(8,128)S(1)}, u32[]{:S(2)}, u32[]{:S(2)}) collective-permute-start(f32[2,32,512]{2,1,0:T(8,128)S(1)} %get-tuple-element.31.fz_ref), channel_id=1, source_target_pairs={{0,1},{1,0},{2,3},{3,2},{4,5},{5,4},{6,7},{7,6},{8,9},{9,8},{10,11... | collective-permute-start | bytes 393224 | tf_op jit(solution)/shard_map/ppermute | solution.py:279

commit v4 on v3

--- a/solution.py
+++ b/solution.py
@@ -88,27 +88,28 @@
     return (8.0 * third) * (p1 - m1) - third * (p2 - m2)
 
 
-def terms_kernel(occ_ref, states_ref, core_ref, out_ref, occ_held, held, core_held, sems):
+def terms_kernel(groups, occ_ref, states_ref, core_ref, *refs):
+    *outs, occ_held, held, core_held, sems = refs
     rows = held.shape[2]
-    parts = out_ref.shape[0]
+    parts = sum(len(group) for group in groups)
     own = rows // parts
+    me = lax.axis_index("interval")
+    flip = lax.rem(lax.axis_index("slab"), 2)
+    first = pltpu.make_async_copy(occ_ref, occ_held, sems.at[0])
+    first.start()
+    copies = []
     pieces = sems.shape[0] - 4
     per = rows // pieces
-    me = lax.axis_index("interval")
-    flip = lax.rem(lax.axis_index("slab"), 2)
-    first = pltpu.make_async_copy(occ_ref, occ_held, sems.at[pieces + 3])
-    first.start()
-    copies = []
     for k in range(pieces):
         at = pl.ds(k * per, per)
-        copies.append(pltpu.make_async_copy(states_ref.at[:, :, at], held.at[:, :, at], sems.at[k]))
+        copies.append(pltpu.make_async_copy(states_ref.at[:, :, at], held.at[:, :, at], sems.at[4 + k]))
     low = pl.multiple_of(lax.rem(me * own + rows - 8, rows), 8)
     mid = pl.multiple_of(me * own, 8)
     top = pl.multiple_of(lax.rem(me * own + own, rows), 8)
     for k, (start, size, to) in enumerate(((mid, own, 0), (top, 8, own), (low, 8, own + 8))):
         copies.append(
             pltpu.make_async_copy(
-                core_ref.at[:, pl.ds(start, size)], core_held.at[:, pl.ds(to, size)], sems.at[pieces + k]
+                core_ref.at[:, pl.ds(start, size)], core_held.at[:, pl.ds(to, size)], sems.at[1 + k]
             )
         )
     for c in copies:
@@ -116,27 +117,34 @@
     first.wait()
     w0 = occ_held[0].astype(jnp.float32) * (1.0 / denominator)
     w1 = occ_held[1].astype(jnp.float32) * (1.0 / denominator)
-    for k in range(pieces):
-        copies[k].wait()
-        for i in range(k * per // own, (k + 1) * per // own):
-            for p in range(2):
-                to = p ^ flip
-                for r in range(0, own, 8):
-                    a = held[0, p, pl.ds(i * own + r, 8)]
-                    b = held[1, p, pl.ds(i * own + r, 8)]
-                    t = w0 * a * a + w1 * b * b
-                    out_ref[i, to, pl.ds(r, 8)] = t
-                    if r == 0:
-                        out_ref[(i - 1) % parts, to, pl.ds(own, HALO)] = t[:HALO]
-                    if r == own - 8:
-                        out_ref[(i + 1) % parts, to, pl.ds(own + HALO, HALO)] = t[HALO:]
-    for c in copies[pieces:]:
+
+    def term(p, row):
+        at = pl.ds(pl.multiple_of(row, 8), 8)
+        a, b = held[0, p, at], held[1, p, at]
+        return w0 * a * a + w1 * b * b
+
+    for c in copies[:pieces]:
         c.wait()
-    for p in range(2):
-        to = p ^ flip
-        for to_row, size, row in ((0, own, 0), (own, HALO, own), (own + HALO, HALO, own + 8 + HALO)):
-            at = pl.ds(to_row, size)
-            out_ref[me, to, at] = out_ref[me, to, at] + core_held[p, pl.ds(row, size)]
+    places = [(k, out, 2 * j) for group, out in zip(groups, outs) for j, k in enumerate(group)]
+    for k, out, shift in places:
+        i = me ^ k
+        up = lax.rem(i + 1, parts) * own
+        down = lax.rem(i + parts - 1, parts) * own + own - 8
+        if k == 0:
+            for c in copies[pieces:]:
+                c.wait()
+        for p in range(2):
+            to = shift + (p ^ flip)
+            for r in range(0, own, 8):
+                t = term(p, i * own + r)
+                if k == 0:
+                    t = t + core_held[p, pl.ds(r, 8)]
+                out[to, pl.ds(r, 8)] = t
+            t, b = term(p, up), term(p, down)
+            if k == 0:
+                t, b = t + core_held[p, pl.ds(own, 8)], b + core_held[p, pl.ds(own + 8, 8)]
+            out[to, pl.ds(own, HALO)] = t[:HALO]
+            out[to, pl.ds(own + HALO, HALO)] = b[HALO:]
 
 
 def x_slopes(field, slopes):
@@ -242,11 +250,12 @@
     wide = own + 2 * HALO
     block = (planes, wide, cols)
     pieces = 4
-    (terms,) = pl.pallas_call(
-        terms_kernel,
-        out_shape=[pltpu.VMEM((parts, *block), f32)],
+    groups = ((5,), (7,), (3,), (6,), (2,), (4,), (1,), (0,))
+    terms = pl.pallas_call(
+        functools.partial(terms_kernel, groups),
+        out_shape=[pltpu.VMEM((planes * len(group), wide, cols), f32) for group in groups],
         in_specs=[pl.BlockSpec(memory_space=pltpu.HBM)] * 3,
-        out_specs=[pl.BlockSpec(memory_space=pltpu.VMEM)],
+        out_specs=[pl.BlockSpec(memory_space=pltpu.VMEM)] * len(groups),
         scratch_shapes=[
             pltpu.SMEM(occupations.shape, jnp.int32),
             pltpu.VMEM(states.shape, f32),
@@ -256,7 +265,14 @@
         compiler_params=pltpu.CompilerParams(vmem_limit_bytes=VMEM_LIMIT),
         name="terms_kernel",
     )(*[pltpu.with_memory_space_constraint(a, pltpu.HBM) for a in (occupations, states, core_density)])
-    density = jnp.sum(lax.all_to_all(terms, "interval", 0, 0), axis=0)
+    swap = lambda a, k: lax.ppermute(a, "interval", [(i, i ^ k) for i in range(parts)])
+    got = swap(terms[0], 1)
+    other = [swap(terms[1], 6), swap(terms[2], 2)]
+    mine = [swap(terms[3], 6), swap(terms[4], 2)]
+    crossing = terms[6] + other[0] + other[1]
+    across = swap(crossing, 1)
+    mine.append(swap(terms[5] + got, 4))
+    density = terms[7] + mine[0] + mine[1] + mine[2] + across
     chips = slabs // 2
     beside = lambda q, odd: (q + (1 if q % 2 == odd else -1)) % chips
     odd_pairs = [(s, 2 * beside(s // 2, 1) + 1 - s % 2) for s in range(slabs)]

time: 42.2 us -> 36.7 us (0.87)
  blocking collectives: 22.8 us -> 0 us
  starting transfers between devices: 10.5 us -> 21.6 us
  waiting for transfers between devices: 4.73 us -> 10.8 us
    all_to_all x1 -> x0, blocking collectives: 22.8 us -> none  [shards(): density = jnp.sum(lax.all_to_all(terms, 'interval', 0, 0), axis=0)]
    ppermute x0 -> x7, starting transfers between devices: none -> 9.89 us  [shards(): lax.ppermute(a, 'interval', [(i, i ^ k) for i in range(parts)])]
    ppermute x0 -> x7, waiting for transfers between devices: none -> 6.79 us  [shards(): lax.ppermute(a, 'interval', [(i, i ^ k) for i in range(parts)])]
    ppermute x1, starting transfers between devices: 9.83 us -> 6.37 us  [shards(): from_odd = lax.ppermute(density, 'slab', odd_pairs)]
    ppermute x1, starting transfers between devices: 0.01 us -> 3.38 us  [shards(): from_even = lax.ppermute(density, 'slab', even_pairs)]
    ppermute x1, waiting for transfers between devices: 1.74 us -> 0.01 us  [shards(): from_even = lax.ppermute(density, 'slab', even_pairs)]
    ppermute x1, starting transfers between devices: 0.01 us -> 1.02 us  [shards(): mate = lax.ppermute(density, 'slab', mates)]
    ppermute x1, starting transfers between devices: 0.09 us -> 0.82 us  [shards(): far = lax.ppermute(other, 'slab', mates)]
  transfers between devices with their start and end apart: 5 -> 12, of which waited for: 3 -> 6; matrix products, arithmetic and copies ran while one was open for 0% -> 0% of each run, Pallas kernels for 3% -> 3%
where the time goes in v4:
time: 36.7 us; the launch traced here: 36.6 us
  starting transfers between devices  21.6 us (59%)
  waiting for transfers between devices  10.8 us (29%)
  Pallas kernels  3.99 us (11%)
    ppermute x7, starting transfers between devices, shards(): lax.ppermute(a, 'interval', [(i, i ^ k) for i in range(parts)])  9.89 us
    ppermute x7, waiting for transfers between devices, shards(): lax.ppermute(a, 'interval', [(i, i ^ k) for i in range(parts)])  6.79 us
    ppermute x1, starting transfers between devices, shards(): from_odd = lax.ppermute(density, 'slab', odd_pairs)  6.37 us
    ppermute x1, starting transfers between devices, shards(): from_even = lax.ppermute(density, 'slab', even_pairs)  3.38 us
    ppermute x1, waiting for transfers between devices, shards(): from_odd = lax.ppermute(density, 'slab', odd_pairs)  3.31 us
    pallas_call x4, Pallas kernels, call(): pl.pallas_call(kernel, out_shape=[jax.ShapeDtypeStruct(o, f32) if out_hbm...  2.1 us
    pallas_call x1, Pallas kernels, shards(): pl.pallas_call(functools.partial(terms_kernel, groups), out_shape=[pltpu....  1.89 us
    ppermute x1, starting transfers between devices, shards(): mate = lax.ppermute(density, 'slab', mates)  1.02 us
  transfers between devices with their start and end apart: 12, of which 6 were waited for; matrix products, arithmetic and copies ran while one was open for 0% of the time, Pallas kernels for 3%

profile of v4, /device:TPU:1, one launch (start us, length us, event | category | flops | bytes accessed | tf_op | source)
XLA Modules:
  0.0 36.6 jit_solution(731128849508648720)
XLA Ops:
  0.0 1.9 %terms_kernel.1 = (f32[2,40,512]{2,1,0:T(8,128)S(1)}, f32[2,40,512]{2,1,0:T(8,128)S(1)}, f32[2,40,512]{2,1,0:T(8,128)S(1)}, f32[2,40,512]{2,1,0:T(8,128)S(1)}, f...) custom-call(s32[2]{0:T(128)} %occ_ref.1, ...), custom_call_target="tpu_custom_call" | custom-call | tf_op jit(solution)/shard_map/terms_kernel/pallas_call | solution.py:254
  1.9 2.2 %collective-permute-start.2 = (f32[2,40,512]{2,1,0:T(8,128)S(1)}, f32[2,40,512]{2,1,0:T(8,128)S(1)}, u32[]{:S(2)}, u32[]{:S(2)}) collective-permute-start(f32[2,40,512]{2,1,0:T(8,128)S(1)} %get-tuple-element.36), channel_id=1, source_target_pairs={{0,32},{32,0},{64,96},{96,64},{128,160},{160,128},{192,224},{224,1... | collective-permute-start | bytes 491528 | tf_op jit(solution)/shard_map/ppermute | solution.py:268
  4.1 2.5 %collective-permute-start.4 = (f32[2,40,512]{2,1,0:T(8,128)S(1)}, f32[2,40,512]{2,1,0:T(8,128)S(1)}, u32[]{:S(2)}, u32[]{:S(2)}) collective-permute-start(f32[2,40,512]{2,1,0:T(8,128)S(1)} %get-tuple-element.38), channel_id=1, source_target_pairs={{0,192},{32,224},{64,128},{96,160},{128,64},{160,96},{192,0},{224,... | collective-permute-start | bytes 491528 | tf_op jit(solution)/shard_map/ppermute | solution.py:268
  6.6 0.0 collective-permute-start.5
  6.6 0.8 %collective-permute-start = (f32[2,40,512]{2,1,0:T(8,128)S(1)}, f32[2,40,512]{2,1,0:T(8,128)S(1)}, u32[]{:S(2)}, u32[]{:S(2)}) collective-permute-start(f32[2,40,512]{2,1,0:T(8,128)S(1)} %get-tuple-element.33), channel_id=1, source_target_pairs={{0,192},{32,224},{64,128},{96,160},{128,64},{160,96},{192,0},{224,... | collective-permute-start | bytes 491528 | tf_op jit(solution)/shard_map/ppermute | solution.py:268
  7.4 0.7 %collective-permute-start.1 = (f32[2,40,512]{2,1,0:T(8,128)S(1)}, f32[2,40,512]{2,1,0:T(8,128)S(1)}, u32[]{:S(2)}, u32[]{:S(2)}) collective-permute-start(f32[2,40,512]{2,1,0:T(8,128)S(1)} %get-tuple-element.34), channel_id=1, source_target_pairs={{0,64},{32,96},{64,0},{96,32},{128,192},{160,224},{192,128},{224,1... | collective-permute-start | bytes 491528 | tf_op jit(solution)/shard_map/ppermute | solution.py:268
  8.1 0.0 collective-permute-done.2
  8.1 2.6 %collective-permute-start.3 = (f32[2,40,512]{2,1,0:T(8,128)S(1)}, f32[2,40,512]{2,1,0:T(8,128)S(1)}, u32[]{:S(2)}, u32[]{:S(2)}) collective-permute-start(f32[2,40,512]{2,1,0:T(8,128)S(1)} %add.27), channel_id=1, source_target_pairs={{0,128},{32,160},{64,192},{96,224},{128,0},{160,32},{192,64},{224,... | collective-permute-start | bytes 491528 | tf_op jit(solution)/shard_map/ppermute | solution.py:268
  10.7 0.0 collective-permute-done.4
  10.8 0.3 collective-permute-done.5
  11.1 1.1 %collective-permute-start.6 = (f32[2,40,512]{2,1,0:T(8,128)S(1)}, f32[2,40,512]{2,1,0:T(8,128)S(1)}, u32[]{:S(2)}, u32[]{:S(2)}) collective-permute-start(f32[2,40,512]{2,1,0:T(8,128)S(1)} %add_add_fusion), channel_id=1, source_target_pairs={{0,32},{32,0},{64,96},{96,64},{128,160},{160,128},{192,224},{224,1... | collective-permute-start | bytes 491528 | tf_op jit(solution)/shard_map/ppermute | solution.py:268
  12.2 1.8 %collective-permute-done = f32[2,40,512]{2,1,0:T(8,128)S(1)} collective-permute-done((f32[2,40,512]{2,1,0:T(8,128)S(1)}, f32[2,40,512]{2,1,0:T(8,128)S(1)}, u32[]{:S(2)}, u32[]{:S(2)}) %collective-permute-start) | collective-permute-done | bytes 163872 | tf_op jit(solution)/shard_map/ppermute | solution.py:268
  14.0 0.5 %collective-permute-done.1 = f32[2,40,512]{2,1,0:T(8,128)S(1)} collective-permute-done((f32[2,40,512]{2,1,0:T(8,128)S(1)}, f32[2,40,512]{2,1,0:T(8,128)S(1)}, u32[]{:S(2)}, u32[]{:S(2)}) %collective-permute-start.1) | collective-permute-done | bytes 163872 | tf_op jit(solution)/shard_map/ppermute | solution.py:268
  14.5 4.1 %collective-permute-done.3 = f32[2,40,512]{2,1,0:T(8,128)S(1)} collective-permute-done((f32[2,40,512]{2,1,0:T(8,128)S(1)}, f32[2,40,512]{2,1,0:T(8,128)S(1)}, u32[]{:S(2)}, u32[]{:S(2)}) %collective-permute-start.3) | collective-permute-done | bytes 163872 | tf_op jit(solution)/shard_map/ppermute | solution.py:268
  18.7 0.0 collective-permute-done.6
  18.7 0.1 add_add_fusion.1.s_ref
  18.7 3.4 %collective-permute-start.8 = (f32[2,40,512]{2,1,0:T(8,128)S(1)}, f32[2,40,512]{2,1,0:T(8,128)S(1)}, u32[]{:S(2)}, u32[]{:S(2)}) collective-permute-start(f32[2,40,512]{2,1,0:T(8,128)S(1)} %add_add_fusion.1.s_ref), channel_id=1, source_target_pairs={{0,3},{1,2},{2,1},{3,0},{4,7},{5,6},{6,5},{7,4},{8,11},{9,10},{10,... | collective-permute-start | bytes 491528 | tf_op jit(solution)/shard_map/ppermute | solution.py:281
  22.1 6.4 %collective-permute-start.7 = (f32[2,40,512]{2,1,0:T(8,128)S(1)}, f32[2,40,512]{2,1,0:T(8,128)S(1)}, u32[]{:S(2)}, u32[]{:S(2)}) collective-permute-start(f32[2,40,512]{2,1,0:T(8,128)S(1)} %add_add_fusion.1.s_ref), channel_id=1, source_target_pairs={{0,31},{1,30},{2,5},{3,4},{4,3},{5,2},{6,9},{7,8},{8,7},{9,6},{10,... | collective-permute-start | bytes 491528 | tf_op jit(solution)/shard_map/ppermute | solution.py:282
  28.5 1.0 %collective-permute-start.10 = (f32[2,40,512]{2,1,0:T(8,128)S(1)}, f32[2,40,512]{2,1,0:T(8,128)S(1)}, u32[]{:S(2)}, u32[]{:S(2)}) collective-permute-start(f32[2,40,512]{2,1,0:T(8,128)S(1)} %add_add_fusion.1.s_ref), channel_id=1, source_target_pairs={{0,1},{1,0},{2,3},{3,2},{4,5},{5,4},{6,7},{7,6},{8,9},{9,8},{10,11... | collective-permute-start | bytes 491528 | tf_op jit(solution)/shard_map/ppermute | solution.py:283
  29.5 0.4 %own_kernel.1 = (f32[2,40,512]{2,1,0:T(8,128)S(1)}, f32[2,40,512]{2,1,0:T(8,128)S(1)}, f32[2,40,512]{2,1,0:T(8,128)S(1)}, f32[2,40,512]{2,1,0:T(8,128)S(1)}, f32...) custom-call(f32[2,40,512]{2,1,0:T(8,128)S(1)} %add_add_fusion.1.s_ref), custom_call_target="tpu_custom_call" | custom-call | flops 100000000 | bytes 983040 | tf_op jit(solution)/shard_map/own_kernel/pallas_call | solution.py:230
  29.9 0.0 collective-permute-done.8
  29.9 3.3 %collective-permute-done.7 = f32[2,40,512]{2,1,0:T(8,128)S(1)} collective-permute-done((f32[2,40,512]{2,1,0:T(8,128)S(1)}, f32[2,40,512]{2,1,0:T(8,128)S(1)}, u32[]{:S(2)}, u32[]{:S(2)}) %collective-permute-start.7) | collective-permute-done | bytes 163872 | tf_op jit(solution)/shard_map/ppermute | solution.py:282
  33.2 0.8 %collective-permute-start.9 = (f32[2,32,512]{2,1,0:T(8,128)S(1)}, f32[2,32,512]{2,1,0:T(8,128)S(1)}, u32[]{:S(2)}, u32[]{:S(2)}) collective-permute-start(f32[2,32,512]{2,1,0:T(8,128)S(1)} %slice_select_fusion), channel_id=1, source_target_pairs={{0,1},{1,0},{2,3},{3,2},{4,5},{5,4},{6,7},{7,6},{8,9},{9,8},{10,11... | collective-permute-start | bytes 393224 | tf_op jit(solution)/shard_map/ppermute | solution.py:290
  34.1 0.0 collective-permute-done.10.m_ref
  34.1 0.2 flux_kernel.1
  34.3 0.1 collective-permute-start.11
  34.4 0.6 %flat_kernel.1 = (f32[2,32,512]{2,1,0:T(8,128)S(1)}, f32[2,32,512]{2,1,0:T(8,128)S(1)}, f32[2,32,512]{2,1,0:T(8,128)S(1)}, f32[2,32,512]{2,1,0:T(8,128)S(1)}) custom-call(f32[2,40,512]{2,1,0:T(8,128)S(1)} %add_add_fusion.1.s_ref, f32[2,40,512]{2,1,0:T(8,128)S(1)} %broadcast_select_fusion.n_ref, f32[2,40,512]{2,1,0:T(8,128)S(1)} %get-tuple-element.43.w_ref, ...), custom_call_target="tpu_custom_call" | custom-call | flops 100000000 | bytes 524288 | tf_op jit(solution)/shard_map/flat_kernel/pallas_call | solution.py:230
  35.0 0.0 collective-permute-done.9.b_ref
  35.1 0.7 %collective-permute-done.11.fm_ref = f32[2,32,512]{2,1,0:T(8,128)S(1)} collective-permute-done((f32[2,32,512]{2,1,0:T(8,128)S(1)}, f32[2,32,512]{2,1,0:T(8,128)S(1)}, u32[]{:S(2)}, u32[]{:S(2)}) %collective-permute-start.11) | collective-permute-done | bytes 131104 | tf_op jit(solution)/shard_map/ppermute | solution.py:295
  35.8 0.9 %last_kernel.1 = f32[2,32,512]{2,1,0:T(8,128)} custom-call(f32[2,40,512]{2,1,0:T(8,128)S(1)} %add_add_fusion.1.s_ref, f32[2,40,512]{2,1,0:T(8,128)S(1)} %broadcast_select_fusion.n_ref, f32[2,32,512]{2,1,0:T(8,128)S(1)} %collective-permute-done.9.b_ref, f32[2,32,512]{2,1,0:T(8,128)S(1)} %get-tuple-element.54.part_ref, ...), custom_call_target="tpu_custom_call" | custom-call | bytes 131072 | tf_op jit(solution)/shard_map/last_kernel/pallas_call | solution.py:230
  (4 shorter events, 0.1 us)
Async XLA Ops:
  1.9 6.2 %collective-permute-start.2 = (f32[2,40,512]{2,1,0:T(8,128)S(1)}, f32[2,40,512]{2,1,0:T(8,128)S(1)}, u32[]{:S(2)}, u32[]{:S(2)}) collective-permute-start(f32[2,40,512]{2,1,0:T(8,128)S(1)} %get-tuple-element.36), channel_id=1, source_target_pairs={{0,32},{32,0},{64,96},{96,64},{128,160},{160,128},{192,224},{224,1... | collective-permute-start | bytes 491528 | tf_op jit(solution)/shard_map/ppermute | solution.py:268
  4.1 6.6 %collective-permute-start.4 = (f32[2,40,512]{2,1,0:T(8,128)S(1)}, f32[2,40,512]{2,1,0:T(8,128)S(1)}, u32[]{:S(2)}, u32[]{:S(2)}) collective-permute-start(f32[2,40,512]{2,1,0:T(8,128)S(1)} %get-tuple-element.38), channel_id=1, source_target_pairs={{0,192},{32,224},{64,128},{96,160},{128,64},{160,96},{192,0},{224,... | collective-permute-start | bytes 491528 | tf_op jit(solution)/shard_map/ppermute | solution.py:268
  6.6 4.5 %collective-permute-start.5 = (f32[2,40,512]{2,1,0:T(8,128)S(1)}, f32[2,40,512]{2,1,0:T(8,128)S(1)}, u32[]{:S(2)}, u32[]{:S(2)}) collective-permute-start(f32[2,40,512]{2,1,0:T(8,128)S(1)} %get-tuple-element.39), channel_id=1, source_target_pairs={{0,64},{32,96},{64,0},{96,32},{128,192},{160,224},{192,128},{224,1... | collective-permute-start | bytes 491528 | tf_op jit(solution)/shard_map/ppermute | solution.py:268
  6.6 7.4 %collective-permute-start = (f32[2,40,512]{2,1,0:T(8,128)S(1)}, f32[2,40,512]{2,1,0:T(8,128)S(1)}, u32[]{:S(2)}, u32[]{:S(2)}) collective-permute-start(f32[2,40,512]{2,1,0:T(8,128)S(1)} %get-tuple-element.33), channel_id=1, source_target_pairs={{0,192},{32,224},{64,128},{96,160},{128,64},{160,96},{192,0},{224,... | collective-permute-start | bytes 491528 | tf_op jit(solution)/shard_map/ppermute | solution.py:268
  7.4 7.1 %collective-permute-start.1 = (f32[2,40,512]{2,1,0:T(8,128)S(1)}, f32[2,40,512]{2,1,0:T(8,128)S(1)}, u32[]{:S(2)}, u32[]{:S(2)}) collective-permute-start(f32[2,40,512]{2,1,0:T(8,128)S(1)} %get-tuple-element.34), channel_id=1, source_target_pairs={{0,64},{32,96},{64,0},{96,32},{128,192},{160,224},{192,128},{224,1... | collective-permute-start | bytes 491528 | tf_op jit(solution)/shard_map/ppermute | solution.py:268
  8.1 10.6 %collective-permute-start.3 = (f32[2,40,512]{2,1,0:T(8,128)S(1)}, f32[2,40,512]{2,1,0:T(8,128)S(1)}, u32[]{:S(2)}, u32[]{:S(2)}) collective-permute-start(f32[2,40,512]{2,1,0:T(8,128)S(1)} %add.27), channel_id=1, source_target_pairs={{0,128},{32,160},{64,192},{96,224},{128,0},{160,32},{192,64},{224,... | collective-permute-start | bytes 491528 | tf_op jit(solution)/shard_map/ppermute | solution.py:268
  11.1 7.6 %collective-permute-start.6 = (f32[2,40,512]{2,1,0:T(8,128)S(1)}, f32[2,40,512]{2,1,0:T(8,128)S(1)}, u32[]{:S(2)}, u32[]{:S(2)}) collective-permute-start(f32[2,40,512]{2,1,0:T(8,128)S(1)} %add_add_fusion), channel_id=1, source_target_pairs={{0,32},{32,0},{64,96},{96,64},{128,160},{160,128},{192,224},{224,1... | collective-permute-start | bytes 491528 | tf_op jit(solution)/shard_map/ppermute | solution.py:268
  18.7 11.2 %collective-permute-start.8 = (f32[2,40,512]{2,1,0:T(8,128)S(1)}, f32[2,40,512]{2,1,0:T(8,128)S(1)}, u32[]{:S(2)}, u32[]{:S(2)}) collective-permute-start(f32[2,40,512]{2,1,0:T(8,128)S(1)} %add_add_fusion.1.s_ref), channel_id=1, source_target_pairs={{0,3},{1,2},{2,1},{3,0},{4,7},{5,6},{6,5},{7,4},{8,11},{9,10},{10,... | collective-permute-start | bytes 491528 | tf_op jit(solution)/shard_map/ppermute | solution.py:281
  22.1 11.1 %collective-permute-start.7 = (f32[2,40,512]{2,1,0:T(8,128)S(1)}, f32[2,40,512]{2,1,0:T(8,128)S(1)}, u32[]{:S(2)}, u32[]{:S(2)}) collective-permute-start(f32[2,40,512]{2,1,0:T(8,128)S(1)} %add_add_fusion.1.s_ref), channel_id=1, source_target_pairs={{0,31},{1,30},{2,5},{3,4},{4,3},{5,2},{6,9},{7,8},{8,7},{9,6},{10,... | collective-permute-start | bytes 491528 | tf_op jit(solution)/shard_map/ppermute | solution.py:282
  28.5 5.6 %collective-permute-start.10 = (f32[2,40,512]{2,1,0:T(8,128)S(1)}, f32[2,40,512]{2,1,0:T(8,128)S(1)}, u32[]{:S(2)}, u32[]{:S(2)}) collective-permute-start(f32[2,40,512]{2,1,0:T(8,128)S(1)} %add_add_fusion.1.s_ref), channel_id=1, source_target_pairs={{0,1},{1,0},{2,3},{3,2},{4,5},{5,4},{6,7},{7,6},{8,9},{9,8},{10,11... | collective-permute-start | bytes 491528 | tf_op jit(solution)/shard_map/ppermute | solution.py:283
  33.2 1.8 %collective-permute-start.9 = (f32[2,32,512]{2,1,0:T(8,128)S(1)}, f32[2,32,512]{2,1,0:T(8,128)S(1)}, u32[]{:S(2)}, u32[]{:S(2)}) collective-permute-start(f32[2,32,512]{2,1,0:T(8,128)S(1)} %slice_select_fusion), channel_id=1, source_target_pairs={{0,1},{1,0},{2,3},{3,2},{4,5},{5,4},{6,7},{7,6},{8,9},{9,8},{10,11... | collective-permute-start | bytes 393224 | tf_op jit(solution)/shard_map/ppermute | solution.py:290
  34.3 1.4 %collective-permute-start.11 = (f32[2,32,512]{2,1,0:T(8,128)S(1)}, f32[2,32,512]{2,1,0:T(8,128)S(1)}, u32[]{:S(2)}, u32[]{:S(2)}) collective-permute-start(f32[2,32,512]{2,1,0:T(8,128)S(1)} %get-tuple-element.47.fz_ref), channel_id=1, source_target_pairs={{0,1},{1,0},{2,3},{3,2},{4,5},{5,4},{6,7},{7,6},{8,9},{9,8},{10,11... | collective-permute-start | bytes 393224 | tf_op jit(solution)/shard_map/ppermute | solution.py:295

commit v5 on v4

--- a/solution.py
+++ b/solution.py
@@ -97,11 +97,10 @@
     flip = lax.rem(lax.axis_index("slab"), 2)
     first = pltpu.make_async_copy(occ_ref, occ_held, sems.at[0])
     first.start()
+    places = [(k, out, 2 * j) for group, out in zip(groups, outs) for j, k in enumerate(group)]
     copies = []
-    pieces = sems.shape[0] - 4
-    per = rows // pieces
-    for k in range(pieces):
-        at = pl.ds(k * per, per)
+    for k, _, _ in places:
+        at = pl.ds(pl.multiple_of((me ^ k) * own, 8), own)
         copies.append(pltpu.make_async_copy(states_ref.at[:, :, at], held.at[:, :, at], sems.at[4 + k]))
     low = pl.multiple_of(lax.rem(me * own + rows - 8, rows), 8)
     mid = pl.multiple_of(me * own, 8)
@@ -123,23 +122,23 @@
         a, b = held[0, p, at], held[1, p, at]
         return w0 * a * a + w1 * b * b
 
-    for c in copies[:pieces]:
-        c.wait()
-    places = [(k, out, 2 * j) for group, out in zip(groups, outs) for j, k in enumerate(group)]
+    for (k, out, shift), copy in zip(places, copies):
+        copy.wait()
+        if k == 0:
+            for c in copies[parts:]:
+                c.wait()
+        for p in range(2):
+            for r in range(0, own, 8):
+                t = term(p, (me ^ k) * own + r)
+                if k == 0:
+                    t = t + core_held[p, pl.ds(r, 8)]
+                out[shift + (p ^ flip), pl.ds(r, 8)] = t
     for k, out, shift in places:
         i = me ^ k
         up = lax.rem(i + 1, parts) * own
         down = lax.rem(i + parts - 1, parts) * own + own - 8
-        if k == 0:
-            for c in copies[pieces:]:
-                c.wait()
         for p in range(2):
             to = shift + (p ^ flip)
-            for r in range(0, own, 8):
-                t = term(p, i * own + r)
-                if k == 0:
-                    t = t + core_held[p, pl.ds(r, 8)]
-                out[to, pl.ds(r, 8)] = t
             t, b = term(p, up), term(p, down)
             if k == 0:
                 t, b = t + core_held[p, pl.ds(own, 8)], b + core_held[p, pl.ds(own + 8, 8)]
@@ -209,9 +208,10 @@
             wn_ref[p, at], an_ref[p, at] = of_density(n, False)
 
 
-def last_kernel(s_ref, n_ref, b_ref, part_ref, wn_ref, an_ref, flat_ref, fz_ref, fm_ref, out_ref):
+def last_kernel(s_ref, n_ref, b_ref, part_ref, wn_ref, an_ref, flat_ref, fz_ref, fm_ref, out_ref, held, sems):
     own = part_ref.shape[1]
     flip = lax.rem(lax.axis_index("slab"), 2)
+    copies = []
     for r in range(0, own, 8):
         at = pl.ds(r, 8)
         s = (s_ref[0, at], s_ref[1, at])
@@ -221,8 +221,12 @@
             f.append(of_gradient(wn_ref[p, at], an_ref[p, at], gz * gz + flat_ref[p, at]) * gz)
         f0, f1 = fz_ref[0, at], fz_ref[1, at]
         f2, f3 = -fm_ref[1, at], -fm_ref[0, at]
-        out_ref[flip, at] = part_ref[0, at] - d_z(f2, f1, f[0], f[1])
-        out_ref[1 - flip, at] = part_ref[1, at] - d_z(f3, f2, f0, f[0])
+        held[flip, at] = part_ref[0, at] - d_z(f2, f1, f[0], f[1])
+        held[1 - flip, at] = part_ref[1, at] - d_z(f3, f2, f0, f[0])
+        copies.append(pltpu.make_async_copy(held.at[:, at], out_ref.at[:, at], sems.at[r // 8]))
+        copies[-1].start()
+    for c in copies:
+        c.wait()
 
 
 def call(kernel, outs, *args, scratch=(), out_hbm=False, flops=0):
@@ -231,7 +235,7 @@
         kernel,
         out_shape=[jax.ShapeDtypeStruct(o, f32) if out_hbm else pltpu.VMEM(o, f32) for o in outs],
         in_specs=[pl.BlockSpec(memory_space=pltpu.VMEM)] * len(args),
-        out_specs=[pl.BlockSpec(memory_space=pltpu.VMEM)] * len(outs),
+        out_specs=[pl.BlockSpec(memory_space=pl.ANY if out_hbm else pltpu.VMEM)] * len(outs),
         scratch_shapes=list(scratch),
         compiler_params=pltpu.CompilerParams(vmem_limit_bytes=VMEM_LIMIT),
         cost_estimate=pl.CostEstimate(
@@ -249,7 +253,6 @@
     own = rows // parts
     wide = own + 2 * HALO
     block = (planes, wide, cols)
-    pieces = 4
     groups = ((5,), (7,), (3,), (6,), (2,), (4,), (1,), (0,))
     terms = pl.pallas_call(
         functools.partial(terms_kernel, groups),
@@ -260,7 +263,7 @@
             pltpu.SMEM(occupations.shape, jnp.int32),
             pltpu.VMEM(states.shape, f32),
             pltpu.VMEM((planes, own + 16, cols), f32),
-            pltpu.SemaphoreType.DMA((pieces + 4,)),
+            pltpu.SemaphoreType.DMA((parts + 4,)),
         ],
         compiler_params=pltpu.CompilerParams(vmem_limit_bytes=VMEM_LIMIT),
         name="terms_kernel",
@@ -278,28 +281,36 @@
     odd_pairs = [(s, 2 * beside(s // 2, 1) + 1 - s % 2) for s in range(slabs)]
     even_pairs = [(s, 2 * beside(s // 2, 0) + 1 - s % 2) for s in range(slabs)]
     mates = [(s, s ^ 1) for s in range(slabs)]
-    from_even = lax.ppermute(density, "slab", even_pairs)
+    low_end = lambda q: q % (chips // 2) < 2
+    first = [pair if low_end(pair[0] // 2) else (pair[0], pair[0]) for pair in even_pairs]
+    last = [(pair[0], pair[0]) if low_end(pair[0] // 2) else pair for pair in even_pairs]
+    from_first = lax.ppermute(density, "slab", first)
     from_odd = lax.ppermute(density, "slab", odd_pairs)
+    from_last = lax.ppermute(density, "slab", last)
     mate = lax.ppermute(density, "slab", mates)
     w, factor, base, change, gx, gy = call(own_kernel, [block] * 6, density, flops=100_000_000)
-    from_odd, from_even, w = lax.optimization_barrier((from_odd, from_even, w))
+    from_last, from_odd, from_first, w = lax.optimization_barrier((from_last, from_odd, from_first, w))
     at = lax.axis_index("slab")
+    at_end = low_end(at // 2)
+    from_even = jnp.where(at_end, from_first, from_last)
     odd_near = lax.rem(at // 2 + at, 2) == 0
     near = jnp.where(odd_near, from_odd, from_even)
     other = jnp.where(odd_near, from_even, from_odd)[:, :own]
-    far = lax.ppermute(other, "slab", mates)
     kept = (planes, own, cols)
     fz, g, twice = call(
         flux_kernel, [kept, block, block], density, mate, near, w, factor, gx, gy, flops=50_000_000
     )
-    fz_mate = lax.ppermute(fz, "slab", mates)
+    to_mate, other = lax.optimization_barrier((fz, other))
+    far = lax.ppermute(other, "slab", mates)
+    fz_mate = lax.ppermute(to_mate, "slab", mates)
     part, w_n, factor_n, flat_n = call(
         flat_kernel, [kept] * 4, density, near, w, factor, base, change, gx, gy, g, twice,
         scratch=[pltpu.VMEM(block, f32)] * 2, flops=100_000_000,
     )
     far, fz_mate, part = lax.optimization_barrier((far, fz_mate, part))
     (out,) = call(
-        last_kernel, [kept], density, near, far, part, w_n, factor_n, flat_n, fz, fz_mate, out_hbm=True
+        last_kernel, [kept], density, near, far, part, w_n, factor_n, flat_n, fz, fz_mate, out_hbm=True,
+        scratch=[pltpu.VMEM(kept, f32), pltpu.SemaphoreType.DMA((own // 8,))],
     )
     return out
 

time: 36.7 us -> 35.2 us (0.959)
  waiting for transfers between devices: 10.8 us -> 9.33 us
    ppermute x2 -> x3, starting transfers between devices: 3.49 us -> 6.36 us  [the longest x1 5.2 us: shards(): from_first = lax.ppermute(density, 'slab', first)]
    ppermute x1, starting transfers between devices: 6.37 us -> 5.12 us  [shards(): from_odd = lax.ppermute(density, 'slab', odd_pairs)]
    ppermute x1, waiting for transfers between devices: 3.31 us -> 2.13 us  [shards(): from_odd = lax.ppermute(density, 'slab', odd_pairs)]
    ppermute x1, starting transfers between devices: 1.02 us -> 0.09 us  [shards(): mate = lax.ppermute(density, 'slab', mates)]
    ppermute x1, starting transfers between devices: 0.82 us -> 0.09 us  [shards(): far = lax.ppermute(other, 'slab', mates)]
    ppermute x2 -> x3, waiting for transfers between devices: 0.7 us -> 0.19 us  [the longest x1 0.19 us: shards(): fz_mate = lax.ppermute(to_mate, 'slab', mates)]
  transfers between devices with their start and end apart: 12 -> 13, of which waited for: 6 -> 7; matrix products, arithmetic and copies ran while one was open for 0% -> 0% of each run, Pallas kernels for 3% -> 3%
where the time goes in v5:
time: 35.2 us; the launch traced here: 35.1 us
  starting transfers between devices  21.6 us (61%)
  waiting for transfers between devices  9.33 us (27%)
  Pallas kernels  3.86 us (11%)
    ppermute x7, starting transfers between devices, shards(): lax.ppermute(a, 'interval', [(i, i ^ k) for i in range(parts)])  9.89 us
    ppermute x7, waiting for transfers between devices, shards(): lax.ppermute(a, 'interval', [(i, i ^ k) for i in range(parts)])  6.79 us
    ppermute x1, starting transfers between devices, shards(): from_first = lax.ppermute(density, 'slab', first)  5.2 us
    ppermute x1, starting transfers between devices, shards(): from_odd = lax.ppermute(density, 'slab', odd_pairs)  5.12 us
    ppermute x1, waiting for transfers between devices, shards(): from_odd = lax.ppermute(density, 'slab', odd_pairs)  2.13 us
    pallas_call x4, Pallas kernels, call(): pl.pallas_call(kernel, out_shape=[jax.ShapeDtypeStruct(o, f32) if out_hbm...  2.1 us
    pallas_call x1, Pallas kernels, shards(): pl.pallas_call(functools.partial(terms_kernel, groups), out_shape=[pltpu....  1.76 us
  transfers between devices with their start and end apart: 13, of which 7 were waited for; matrix products, arithmetic and copies ran while one was open for 0% of the time, Pallas kernels for 3%

profile of v5, /device:TPU:1, one launch (start us, length us, event | category | flops | bytes accessed | tf_op | source)
XLA Modules:
  0.0 35.1 jit_solution(14202202424589789992)
XLA Ops:
  0.0 1.8 %terms_kernel.1 = (f32[2,40,512]{2,1,0:T(8,128)S(1)}, f32[2,40,512]{2,1,0:T(8,128)S(1)}, f32[2,40,512]{2,1,0:T(8,128)S(1)}, f32[2,40,512]{2,1,0:T(8,128)S(1)}, f...) custom-call(s32[2]{0:T(128)} %occ_ref.1, ...), custom_call_target="tpu_custom_call" | custom-call | tf_op jit(solution)/shard_map/terms_kernel/pallas_call | solution.py:257
  1.8 2.2 %collective-permute-start.2 = (f32[2,40,512]{2,1,0:T(8,128)S(1)}, f32[2,40,512]{2,1,0:T(8,128)S(1)}, u32[]{:S(2)}, u32[]{:S(2)}) collective-permute-start(f32[2,40,512]{2,1,0:T(8,128)S(1)} %get-tuple-element.39), channel_id=1, source_target_pairs={{0,32},{32,0},{64,96},{96,64},{128,160},{160,128},{192,224},{224,1... | collective-permute-start | bytes 491528 | tf_op jit(solution)/shard_map/ppermute | solution.py:271
  4.0 2.5 %collective-permute-start.4 = (f32[2,40,512]{2,1,0:T(8,128)S(1)}, f32[2,40,512]{2,1,0:T(8,128)S(1)}, u32[]{:S(2)}, u32[]{:S(2)}) collective-permute-start(f32[2,40,512]{2,1,0:T(8,128)S(1)} %get-tuple-element.41), channel_id=1, source_target_pairs={{0,192},{32,224},{64,128},{96,160},{128,64},{160,96},{192,0},{224,... | collective-permute-start | bytes 491528 | tf_op jit(solution)/shard_map/ppermute | solution.py:271
  6.5 0.0 collective-permute-start.5
  6.5 0.8 %collective-permute-start = (f32[2,40,512]{2,1,0:T(8,128)S(1)}, f32[2,40,512]{2,1,0:T(8,128)S(1)}, u32[]{:S(2)}, u32[]{:S(2)}) collective-permute-start(f32[2,40,512]{2,1,0:T(8,128)S(1)} %get-tuple-element.36), channel_id=1, source_target_pairs={{0,192},{32,224},{64,128},{96,160},{128,64},{160,96},{192,0},{224,... | collective-permute-start | bytes 491528 | tf_op jit(solution)/shard_map/ppermute | solution.py:271
  7.3 0.7 %collective-permute-start.1 = (f32[2,40,512]{2,1,0:T(8,128)S(1)}, f32[2,40,512]{2,1,0:T(8,128)S(1)}, u32[]{:S(2)}, u32[]{:S(2)}) collective-permute-start(f32[2,40,512]{2,1,0:T(8,128)S(1)} %get-tuple-element.37), channel_id=1, source_target_pairs={{0,64},{32,96},{64,0},{96,32},{128,192},{160,224},{192,128},{224,1... | collective-permute-start | bytes 491528 | tf_op jit(solution)/shard_map/ppermute | solution.py:271
  7.9 0.0 collective-permute-done.2
  8.0 2.6 %collective-permute-start.3 = (f32[2,40,512]{2,1,0:T(8,128)S(1)}, f32[2,40,512]{2,1,0:T(8,128)S(1)}, u32[]{:S(2)}, u32[]{:S(2)}) collective-permute-start(f32[2,40,512]{2,1,0:T(8,128)S(1)} %add.31), channel_id=1, source_target_pairs={{0,128},{32,160},{64,192},{96,224},{128,0},{160,32},{192,64},{224,... | collective-permute-start | bytes 491528 | tf_op jit(solution)/shard_map/ppermute | solution.py:271
  10.6 0.0 collective-permute-done.4
  10.6 0.3 collective-permute-done.5
  11.0 1.1 %collective-permute-start.6 = (f32[2,40,512]{2,1,0:T(8,128)S(1)}, f32[2,40,512]{2,1,0:T(8,128)S(1)}, u32[]{:S(2)}, u32[]{:S(2)}) collective-permute-start(f32[2,40,512]{2,1,0:T(8,128)S(1)} %add_add_fusion), channel_id=1, source_target_pairs={{0,32},{32,0},{64,96},{96,64},{128,160},{160,128},{192,224},{224,1... | collective-permute-start | bytes 491528 | tf_op jit(solution)/shard_map/ppermute | solution.py:271
  12.0 1.8 %collective-permute-done = f32[2,40,512]{2,1,0:T(8,128)S(1)} collective-permute-done((f32[2,40,512]{2,1,0:T(8,128)S(1)}, f32[2,40,512]{2,1,0:T(8,128)S(1)}, u32[]{:S(2)}, u32[]{:S(2)}) %collective-permute-start) | collective-permute-done | bytes 163872 | tf_op jit(solution)/shard_map/ppermute | solution.py:271
  13.9 0.5 %collective-permute-done.1 = f32[2,40,512]{2,1,0:T(8,128)S(1)} collective-permute-done((f32[2,40,512]{2,1,0:T(8,128)S(1)}, f32[2,40,512]{2,1,0:T(8,128)S(1)}, u32[]{:S(2)}, u32[]{:S(2)}) %collective-permute-start.1) | collective-permute-done | bytes 163872 | tf_op jit(solution)/shard_map/ppermute | solution.py:271
  14.4 4.1 %collective-permute-done.3 = f32[2,40,512]{2,1,0:T(8,128)S(1)} collective-permute-done((f32[2,40,512]{2,1,0:T(8,128)S(1)}, f32[2,40,512]{2,1,0:T(8,128)S(1)}, u32[]{:S(2)}, u32[]{:S(2)}) %collective-permute-start.3) | collective-permute-done | bytes 163872 | tf_op jit(solution)/shard_map/ppermute | solution.py:271
  18.5 0.0 collective-permute-done.6
  18.5 0.1 add_add_fusion.1.s_ref
  18.6 5.2 %collective-permute-start.9 = (f32[2,40,512]{2,1,0:T(8,128)S(1)}, f32[2,40,512]{2,1,0:T(8,128)S(1)}, u32[]{:S(2)}, u32[]{:S(2)}) collective-permute-start(f32[2,40,512]{2,1,0:T(8,128)S(1)} %add_add_fusion.1.s_ref), channel_id=1, source_target_pairs={{0,3},{1,2},{2,1},{3,0},{4,4},{5,5},{6,6},{7,7},{8,8},{9,9},{10,10... | collective-permute-start | bytes 491528 | tf_op jit(solution)/shard_map/ppermute | solution.py:287
  23.8 5.1 %collective-permute-start.8 = (f32[2,40,512]{2,1,0:T(8,128)S(1)}, f32[2,40,512]{2,1,0:T(8,128)S(1)}, u32[]{:S(2)}, u32[]{:S(2)}) collective-permute-start(f32[2,40,512]{2,1,0:T(8,128)S(1)} %add_add_fusion.1.s_ref), channel_id=1, source_target_pairs={{0,31},{1,30},{2,5},{3,4},{4,3},{5,2},{6,9},{7,8},{8,7},{9,6},{10,... | collective-permute-start | bytes 491528 | tf_op jit(solution)/shard_map/ppermute | solution.py:288
  28.9 0.7 %collective-permute-start.7 = (f32[2,40,512]{2,1,0:T(8,128)S(1)}, f32[2,40,512]{2,1,0:T(8,128)S(1)}, u32[]{:S(2)}, u32[]{:S(2)}) collective-permute-start(f32[2,40,512]{2,1,0:T(8,128)S(1)} %add_add_fusion.1.s_ref), channel_id=1, source_target_pairs={{0,0},{1,1},{2,2},{3,3},{4,7},{5,6},{6,5},{7,4},{8,11},{9,10},{10,... | collective-permute-start | bytes 491528 | tf_op jit(solution)/shard_map/ppermute | solution.py:289
  29.6 0.1 collective-permute-start.10
  29.7 0.4 %own_kernel.1 = (f32[2,40,512]{2,1,0:T(8,128)S(1)}, f32[2,40,512]{2,1,0:T(8,128)S(1)}, f32[2,40,512]{2,1,0:T(8,128)S(1)}, f32[2,40,512]{2,1,0:T(8,128)S(1)}, f32...) custom-call(f32[2,40,512]{2,1,0:T(8,128)S(1)} %add_add_fusion.1.s_ref), custom_call_target="tpu_custom_call" | custom-call | flops 100000000 | bytes 983040 | tf_op jit(solution)/shard_map/own_kernel/pallas_call | solution.py:234
  30.1 0.0 collective-permute-done.9
  30.1 2.1 %collective-permute-done.8 = f32[2,40,512]{2,1,0:T(8,128)S(1)} collective-permute-done((f32[2,40,512]{2,1,0:T(8,128)S(1)}, f32[2,40,512]{2,1,0:T(8,128)S(1)}, u32[]{:S(2)}, u32[]{:S(2)}) %collective-permute-start.8) | collective-permute-done | bytes 163872 | tf_op jit(solution)/shard_map/ppermute | solution.py:288
  32.2 0.0 collective-permute-done.7
  32.3 0.0 collective-permute-done.10.m_ref
  32.3 0.2 flux_kernel.1
  32.6 0.1 collective-permute-start.11
  32.7 0.5 %collective-permute-start.12 = (f32[2,32,512]{2,1,0:T(8,128)S(1)}, f32[2,32,512]{2,1,0:T(8,128)S(1)}, u32[]{:S(2)}, u32[]{:S(2)}) collective-permute-start(f32[2,32,512]{2,1,0:T(8,128)S(1)} %get-tuple-element.53.fz_ref), channel_id=1, source_target_pairs={{0,1},{1,0},{2,3},{3,2},{4,5},{5,4},{6,7},{7,6},{8,9},{9,8},{10,11... | collective-permute-start | bytes 393224 | tf_op jit(solution)/shard_map/ppermute | solution.py:305
  33.2 0.6 %flat_kernel.1 = (f32[2,32,512]{2,1,0:T(8,128)S(1)}, f32[2,32,512]{2,1,0:T(8,128)S(1)}, f32[2,32,512]{2,1,0:T(8,128)S(1)}, f32[2,32,512]{2,1,0:T(8,128)S(1)}) custom-call(f32[2,40,512]{2,1,0:T(8,128)S(1)} %add_add_fusion.1.s_ref, f32[2,40,512]{2,1,0:T(8,128)S(1)} %get-tuple-element.65.n_ref, f32[2,40,512]{2,1,0:T(8,128)S(1)} %get-tuple-element.47.w_ref, ...), custom_call_target="tpu_custom_call" | custom-call | flops 100000000 | bytes 524288 | tf_op jit(solution)/shard_map/flat_kernel/pallas_call | solution.py:234
  33.8 0.2 collective-permute-done.11.b_ref
  34.0 0.2 collective-permute-done.12.fm_ref
  34.2 0.9 %last_kernel.1 = f32[2,32,512]{2,1,0:T(8,128)} custom-call(f32[2,40,512]{2,1,0:T(8,128)S(1)} %add_add_fusion.1.s_ref, f32[2,40,512]{2,1,0:T(8,128)S(1)} %get-tuple-element.65.n_ref, f32[2,32,512]{2,1,0:T(8,128)S(1)} %collective-permute-done.11.b_ref, f32[2,32,512]{2,1,0:T(8,128)S(1)} %get-tuple-element.60.part_ref, ...), custom_call_target="tpu_custom_call" | custom-call | bytes 131072 | tf_op jit(solution)/shard_map/last_kernel/pallas_call | solution.py:234
  (4 shorter events, 0.1 us)
Async XLA Ops:
  1.8 6.2 %collective-permute-start.2 = (f32[2,40,512]{2,1,0:T(8,128)S(1)}, f32[2,40,512]{2,1,0:T(8,128)S(1)}, u32[]{:S(2)}, u32[]{:S(2)}) collective-permute-start(f32[2,40,512]{2,1,0:T(8,128)S(1)} %get-tuple-element.39), channel_id=1, source_target_pairs={{0,32},{32,0},{64,96},{96,64},{128,160},{160,128},{192,224},{224,1... | collective-permute-start | bytes 491528 | tf_op jit(solution)/shard_map/ppermute | solution.py:271
  4.0 6.6 %collective-permute-start.4 = (f32[2,40,512]{2,1,0:T(8,128)S(1)}, f32[2,40,512]{2,1,0:T(8,128)S(1)}, u32[]{:S(2)}, u32[]{:S(2)}) collective-permute-start(f32[2,40,512]{2,1,0:T(8,128)S(1)} %get-tuple-element.41), channel_id=1, source_target_pairs={{0,192},{32,224},{64,128},{96,160},{128,64},{160,96},{192,0},{224,... | collective-permute-start | bytes 491528 | tf_op jit(solution)/shard_map/ppermute | solution.py:271
  6.5 4.5 %collective-permute-start.5 = (f32[2,40,512]{2,1,0:T(8,128)S(1)}, f32[2,40,512]{2,1,0:T(8,128)S(1)}, u32[]{:S(2)}, u32[]{:S(2)}) collective-permute-start(f32[2,40,512]{2,1,0:T(8,128)S(1)} %get-tuple-element.42), channel_id=1, source_target_pairs={{0,64},{32,96},{64,0},{96,32},{128,192},{160,224},{192,128},{224,1... | collective-permute-start | bytes 491528 | tf_op jit(solution)/shard_map/ppermute | solution.py:271
  6.5 7.4 %collective-permute-start = (f32[2,40,512]{2,1,0:T(8,128)S(1)}, f32[2,40,512]{2,1,0:T(8,128)S(1)}, u32[]{:S(2)}, u32[]{:S(2)}) collective-permute-start(f32[2,40,512]{2,1,0:T(8,128)S(1)} %get-tuple-element.36), channel_id=1, source_target_pairs={{0,192},{32,224},{64,128},{96,160},{128,64},{160,96},{192,0},{224,... | collective-permute-start | bytes 491528 | tf_op jit(solution)/shard_map/ppermute | solution.py:271
  7.3 7.1 %collective-permute-start.1 = (f32[2,40,512]{2,1,0:T(8,128)S(1)}, f32[2,40,512]{2,1,0:T(8,128)S(1)}, u32[]{:S(2)}, u32[]{:S(2)}) collective-permute-start(f32[2,40,512]{2,1,0:T(8,128)S(1)} %get-tuple-element.37), channel_id=1, source_target_pairs={{0,64},{32,96},{64,0},{96,32},{128,192},{160,224},{192,128},{224,1... | collective-permute-start | bytes 491528 | tf_op jit(solution)/shard_map/ppermute | solution.py:271
  8.0 10.6 %collective-permute-start.3 = (f32[2,40,512]{2,1,0:T(8,128)S(1)}, f32[2,40,512]{2,1,0:T(8,128)S(1)}, u32[]{:S(2)}, u32[]{:S(2)}) collective-permute-start(f32[2,40,512]{2,1,0:T(8,128)S(1)} %add.31), channel_id=1, source_target_pairs={{0,128},{32,160},{64,192},{96,224},{128,0},{160,32},{192,64},{224,... | collective-permute-start | bytes 491528 | tf_op jit(solution)/shard_map/ppermute | solution.py:271
  11.0 7.6 %collective-permute-start.6 = (f32[2,40,512]{2,1,0:T(8,128)S(1)}, f32[2,40,512]{2,1,0:T(8,128)S(1)}, u32[]{:S(2)}, u32[]{:S(2)}) collective-permute-start(f32[2,40,512]{2,1,0:T(8,128)S(1)} %add_add_fusion), channel_id=1, source_target_pairs={{0,32},{32,0},{64,96},{96,64},{128,160},{160,128},{192,224},{224,1... | collective-permute-start | bytes 491528 | tf_op jit(solution)/shard_map/ppermute | solution.py:271
  18.6 11.5 %collective-permute-start.9 = (f32[2,40,512]{2,1,0:T(8,128)S(1)}, f32[2,40,512]{2,1,0:T(8,128)S(1)}, u32[]{:S(2)}, u32[]{:S(2)}) collective-permute-start(f32[2,40,512]{2,1,0:T(8,128)S(1)} %add_add_fusion.1.s_ref), channel_id=1, source_target_pairs={{0,3},{1,2},{2,1},{3,0},{4,4},{5,5},{6,6},{7,7},{8,8},{9,9},{10,10... | collective-permute-start | bytes 491528 | tf_op jit(solution)/shard_map/ppermute | solution.py:287
  23.8 8.4 %collective-permute-start.8 = (f32[2,40,512]{2,1,0:T(8,128)S(1)}, f32[2,40,512]{2,1,0:T(8,128)S(1)}, u32[]{:S(2)}, u32[]{:S(2)}) collective-permute-start(f32[2,40,512]{2,1,0:T(8,128)S(1)} %add_add_fusion.1.s_ref), channel_id=1, source_target_pairs={{0,31},{1,30},{2,5},{3,4},{4,3},{5,2},{6,9},{7,8},{8,7},{9,6},{10,... | collective-permute-start | bytes 491528 | tf_op jit(solution)/shard_map/ppermute | solution.py:288
  28.9 3.3 %collective-permute-start.7 = (f32[2,40,512]{2,1,0:T(8,128)S(1)}, f32[2,40,512]{2,1,0:T(8,128)S(1)}, u32[]{:S(2)}, u32[]{:S(2)}) collective-permute-start(f32[2,40,512]{2,1,0:T(8,128)S(1)} %add_add_fusion.1.s_ref), channel_id=1, source_target_pairs={{0,0},{1,1},{2,2},{3,3},{4,7},{5,6},{6,5},{7,4},{8,11},{9,10},{10,... | collective-permute-start | bytes 491528 | tf_op jit(solution)/shard_map/ppermute | solution.py:289
  29.6 2.7 %collective-permute-start.10 = (f32[2,40,512]{2,1,0:T(8,128)S(1)}, f32[2,40,512]{2,1,0:T(8,128)S(1)}, u32[]{:S(2)}, u32[]{:S(2)}) collective-permute-start(f32[2,40,512]{2,1,0:T(8,128)S(1)} %add_add_fusion.1.s_ref), channel_id=1, source_target_pairs={{0,1},{1,0},{2,3},{3,2},{4,5},{5,4},{6,7},{7,6},{8,9},{9,8},{10,11... | collective-permute-start | bytes 491528 | tf_op jit(solution)/shard_map/ppermute | solution.py:290
  32.6 1.4 %collective-permute-start.11 = (f32[2,32,512]{2,1,0:T(8,128)S(1)}, f32[2,32,512]{2,1,0:T(8,128)S(1)}, u32[]{:S(2)}, u32[]{:S(2)}) collective-permute-start(f32[2,32,512]{2,1,0:T(8,128)S(1)} %slice_select_fusion), channel_id=1, source_target_pairs={{0,1},{1,0},{2,3},{3,2},{4,5},{5,4},{6,7},{7,6},{8,9},{9,8},{10,11... | collective-permute-start | bytes 393224 | tf_op jit(solution)/shard_map/ppermute | solution.py:304
  32.7 1.5 %collective-permute-start.12 = (f32[2,32,512]{2,1,0:T(8,128)S(1)}, f32[2,32,512]{2,1,0:T(8,128)S(1)}, u32[]{:S(2)}, u32[]{:S(2)}) collective-permute-start(f32[2,32,512]{2,1,0:T(8,128)S(1)} %get-tuple-element.53.fz_ref), channel_id=1, source_target_pairs={{0,1},{1,0},{2,3},{3,2},{4,5},{5,4},{6,7},{7,6},{8,9},{9,8},{10,11... | collective-permute-start | bytes 393224 | tf_op jit(solution)/shard_map/ppermute | solution.py:305

commit v6 on v5

--- a/solution.py
+++ b/solution.py
@@ -269,13 +269,13 @@
         name="terms_kernel",
     )(*[pltpu.with_memory_space_constraint(a, pltpu.HBM) for a in (occupations, states, core_density)])
     swap = lambda a, k: lax.ppermute(a, "interval", [(i, i ^ k) for i in range(parts)])
-    got = swap(terms[0], 1)
     other = [swap(terms[1], 6), swap(terms[2], 2)]
-    mine = [swap(terms[3], 6), swap(terms[4], 2)]
+    got, to_2 = lax.optimization_barrier((swap(terms[0], 1), terms[4]))
+    far = swap(terms[5] + got, 4)
+    mine = [swap(terms[3], 6), swap(to_2, 2)]
     crossing = terms[6] + other[0] + other[1]
     across = swap(crossing, 1)
-    mine.append(swap(terms[5] + got, 4))
-    density = terms[7] + mine[0] + mine[1] + mine[2] + across
+    density = terms[7] + sum(mine[1:], mine[0]) + far + across
     chips = slabs // 2
     beside = lambda q, odd: (q + (1 if q % 2 == odd else -1)) % chips
     odd_pairs = [(s, 2 * beside(s // 2, 1) + 1 - s % 2) for s in range(slabs)]

time: 35.2 us -> 35.1 us (level)
  waiting for transfers between devices: 9.33 us -> 8.43 us
  starting transfers between devices: 21.6 us -> 22.3 us
    ppermute x7, waiting for transfers between devices: 6.79 us -> 5.88 us  [shards(): lax.ppermute(a, 'interval', [(i, i ^ k) for i in range(parts)])]
    ppermute x7, starting transfers between devices: 9.89 us -> 10.5 us  [shards(): lax.ppermute(a, 'interval', [(i, i ^ k) for i in range(parts)])]
  transfers between devices with their start and end apart: 13 -> 13, of which waited for: 7 -> 5; matrix products, arithmetic and copies ran while one was open for 0% -> 0% of each run, Pallas kernels for 3% -> 3%
where the time goes in v6:
time: 35.1 us; the launch traced here: 34.9 us
  starting transfers between devices  22.3 us (64%)
  waiting for transfers between devices  8.43 us (24%)
  Pallas kernels  3.86 us (11%)
    ppermute x7, starting transfers between devices, shards(): lax.ppermute(a, 'interval', [(i, i ^ k) for i in range(parts)])  10.5 us
    ppermute x7, waiting for transfers between devices, shards(): lax.ppermute(a, 'interval', [(i, i ^ k) for i in range(parts)])  5.88 us
    ppermute x1, starting transfers between devices, shards(): from_first = lax.ppermute(density, 'slab', first)  5.34 us
    ppermute x1, starting transfers between devices, shards(): from_odd = lax.ppermute(density, 'slab', odd_pairs)  5.12 us
    ppermute x1, waiting for transfers between devices, shards(): from_odd = lax.ppermute(density, 'slab', odd_pairs)  2.13 us
    pallas_call x4, Pallas kernels, call(): pl.pallas_call(kernel, out_shape=[jax.ShapeDtypeStruct(o, f32) if out_hbm...  2.1 us
    pallas_call x1, Pallas kernels, shards(): pl.pallas_call(functools.partial(terms_kernel, groups), out_shape=[pltpu....  1.76 us
  transfers between devices with their start and end apart: 13, of which 5 were waited for; matrix products, arithmetic and copies ran while one was open for 0% of the time, Pallas kernels for 3%

profile of v6, /device:TPU:1, one launch (start us, length us, event | category | flops | bytes accessed | tf_op | source)
XLA Modules:
  0.0 34.9 jit_solution(1913818511077632866)
XLA Ops:
  0.0 1.8 %terms_kernel.1 = (f32[2,40,512]{2,1,0:T(8,128)S(1)}, f32[2,40,512]{2,1,0:T(8,128)S(1)}, f32[2,40,512]{2,1,0:T(8,128)S(1)}, f32[2,40,512]{2,1,0:T(8,128)S(1)}, f...) custom-call(s32[2]{0:T(128)} %occ_ref.1, ...), custom_call_target="tpu_custom_call" | custom-call | tf_op jit(solution)/shard_map/terms_kernel/pallas_call | solution.py:257
  1.8 2.2 %collective-permute-start.1 = (f32[2,40,512]{2,1,0:T(8,128)S(1)}, f32[2,40,512]{2,1,0:T(8,128)S(1)}, u32[]{:S(2)}, u32[]{:S(2)}) collective-permute-start(f32[2,40,512]{2,1,0:T(8,128)S(1)} %get-tuple-element.39), channel_id=1, source_target_pairs={{0,32},{32,0},{64,96},{96,64},{128,160},{160,128},{192,224},{224,1... | collective-permute-start | bytes 491528 | tf_op jit(solution)/shard_map/ppermute | solution.py:271
  4.0 2.5 %collective-permute-start.4 = (f32[2,40,512]{2,1,0:T(8,128)S(1)}, f32[2,40,512]{2,1,0:T(8,128)S(1)}, u32[]{:S(2)}, u32[]{:S(2)}) collective-permute-start(f32[2,40,512]{2,1,0:T(8,128)S(1)} %get-tuple-element.45), channel_id=1, source_target_pairs={{0,192},{32,224},{64,128},{96,160},{128,64},{160,96},{192,0},{224,... | collective-permute-start | bytes 491528 | tf_op jit(solution)/shard_map/ppermute | solution.py:271
  6.5 0.0 collective-permute-start.5
  6.5 0.8 %collective-permute-start = (f32[2,40,512]{2,1,0:T(8,128)S(1)}, f32[2,40,512]{2,1,0:T(8,128)S(1)}, u32[]{:S(2)}, u32[]{:S(2)}) collective-permute-start(f32[2,40,512]{2,1,0:T(8,128)S(1)} %get-tuple-element.38), channel_id=1, source_target_pairs={{0,192},{32,224},{64,128},{96,160},{128,64},{160,96},{192,0},{224,... | collective-permute-start | bytes 491528 | tf_op jit(solution)/shard_map/ppermute | solution.py:271
  7.3 0.0 collective-permute-done.1
  7.3 3.3 %collective-permute-start.3 = (f32[2,40,512]{2,1,0:T(8,128)S(1)}, f32[2,40,512]{2,1,0:T(8,128)S(1)}, u32[]{:S(2)}, u32[]{:S(2)}) collective-permute-start(f32[2,40,512]{2,1,0:T(8,128)S(1)} %add.31), channel_id=1, source_target_pairs={{0,128},{32,160},{64,192},{96,224},{128,0},{160,32},{192,64},{224,... | collective-permute-start | bytes 491528 | tf_op jit(solution)/shard_map/ppermute | solution.py:271
  10.6 0.3 collective-permute-start.2
  10.9 0.0 collective-permute-done.4
  10.9 0.0 collective-permute-done.5
  11.0 1.4 %collective-permute-start.6 = (f32[2,40,512]{2,1,0:T(8,128)S(1)}, f32[2,40,512]{2,1,0:T(8,128)S(1)}, u32[]{:S(2)}, u32[]{:S(2)}) collective-permute-start(f32[2,40,512]{2,1,0:T(8,128)S(1)} %add_add_fusion), channel_id=1, source_target_pairs={{0,32},{32,0},{64,96},{96,64},{128,160},{160,128},{192,224},{224,1... | collective-permute-start | bytes 491528 | tf_op jit(solution)/shard_map/ppermute | solution.py:271
  12.4 3.6 %collective-permute-done = f32[2,40,512]{2,1,0:T(8,128)S(1)} collective-permute-done((f32[2,40,512]{2,1,0:T(8,128)S(1)}, f32[2,40,512]{2,1,0:T(8,128)S(1)}, u32[]{:S(2)}, u32[]{:S(2)}) %collective-permute-start) | collective-permute-done | bytes 163872 | tf_op jit(solution)/shard_map/ppermute | solution.py:271
  16.0 0.0 collective-permute-done.3
  16.0 2.3 %collective-permute-done.2 = f32[2,40,512]{2,1,0:T(8,128)S(1)} collective-permute-done((f32[2,40,512]{2,1,0:T(8,128)S(1)}, f32[2,40,512]{2,1,0:T(8,128)S(1)}, u32[]{:S(2)}, u32[]{:S(2)}) %collective-permute-start.2) | collective-permute-done | bytes 163872 | tf_op jit(solution)/shard_map/ppermute | solution.py:271
  18.2 0.0 collective-permute-done.6
  18.2 0.1 add_add_fusion.1.s_ref
  18.3 5.3 %collective-permute-start.9 = (f32[2,40,512]{2,1,0:T(8,128)S(1)}, f32[2,40,512]{2,1,0:T(8,128)S(1)}, u32[]{:S(2)}, u32[]{:S(2)}) collective-permute-start(f32[2,40,512]{2,1,0:T(8,128)S(1)} %add_add_fusion.1.s_ref), channel_id=1, source_target_pairs={{0,3},{1,2},{2,1},{3,0},{4,4},{5,5},{6,6},{7,7},{8,8},{9,9},{10,10... | collective-permute-start | bytes 491528 | tf_op jit(solution)/shard_map/ppermute | solution.py:287
  23.6 5.1 %collective-permute-start.8 = (f32[2,40,512]{2,1,0:T(8,128)S(1)}, f32[2,40,512]{2,1,0:T(8,128)S(1)}, u32[]{:S(2)}, u32[]{:S(2)}) collective-permute-start(f32[2,40,512]{2,1,0:T(8,128)S(1)} %add_add_fusion.1.s_ref), channel_id=1, source_target_pairs={{0,31},{1,30},{2,5},{3,4},{4,3},{5,2},{6,9},{7,8},{8,7},{9,6},{10,... | collective-permute-start | bytes 491528 | tf_op jit(solution)/shard_map/ppermute | solution.py:288
  28.8 0.7 %collective-permute-start.7 = (f32[2,40,512]{2,1,0:T(8,128)S(1)}, f32[2,40,512]{2,1,0:T(8,128)S(1)}, u32[]{:S(2)}, u32[]{:S(2)}) collective-permute-start(f32[2,40,512]{2,1,0:T(8,128)S(1)} %add_add_fusion.1.s_ref), channel_id=1, source_target_pairs={{0,0},{1,1},{2,2},{3,3},{4,7},{5,6},{6,5},{7,4},{8,11},{9,10},{10,... | collective-permute-start | bytes 491528 | tf_op jit(solution)/shard_map/ppermute | solution.py:289
  29.5 0.1 collective-permute-start.10
  29.6 0.4 %own_kernel.1 = (f32[2,40,512]{2,1,0:T(8,128)S(1)}, f32[2,40,512]{2,1,0:T(8,128)S(1)}, f32[2,40,512]{2,1,0:T(8,128)S(1)}, f32[2,40,512]{2,1,0:T(8,128)S(1)}, f32...) custom-call(f32[2,40,512]{2,1,0:T(8,128)S(1)} %add_add_fusion.1.s_ref), custom_call_target="tpu_custom_call" | custom-call | flops 100000000 | bytes 983040 | tf_op jit(solution)/shard_map/own_kernel/pallas_call | solution.py:234
  30.0 0.0 collective-permute-done.9
  30.0 2.1 %collective-permute-done.8 = f32[2,40,512]{2,1,0:T(8,128)S(1)} collective-permute-done((f32[2,40,512]{2,1,0:T(8,128)S(1)}, f32[2,40,512]{2,1,0:T(8,128)S(1)}, u32[]{:S(2)}, u32[]{:S(2)}) %collective-permute-start.8) | collective-permute-done | bytes 163872 | tf_op jit(solution)/shard_map/ppermute | solution.py:288
  32.1 0.0 collective-permute-done.7
  32.2 0.0 collective-permute-done.10.m_ref
  32.2 0.2 flux_kernel.1
  32.4 0.1 collective-permute-start.11
  32.5 0.5 %collective-permute-start.12 = (f32[2,32,512]{2,1,0:T(8,128)S(1)}, f32[2,32,512]{2,1,0:T(8,128)S(1)}, u32[]{:S(2)}, u32[]{:S(2)}) collective-permute-start(f32[2,32,512]{2,1,0:T(8,128)S(1)} %get-tuple-element.57.fz_ref), channel_id=1, source_target_pairs={{0,1},{1,0},{2,3},{3,2},{4,5},{5,4},{6,7},{7,6},{8,9},{9,8},{10,11... | collective-permute-start | bytes 393224 | tf_op jit(solution)/shard_map/ppermute | solution.py:305
  33.0 0.6 %flat_kernel.1 = (f32[2,32,512]{2,1,0:T(8,128)S(1)}, f32[2,32,512]{2,1,0:T(8,128)S(1)}, f32[2,32,512]{2,1,0:T(8,128)S(1)}, f32[2,32,512]{2,1,0:T(8,128)S(1)}) custom-call(f32[2,40,512]{2,1,0:T(8,128)S(1)} %add_add_fusion.1.s_ref, f32[2,40,512]{2,1,0:T(8,128)S(1)} %get-tuple-element.69.n_ref, f32[2,40,512]{2,1,0:T(8,128)S(1)} %get-tuple-element.51.w_ref, ...), custom_call_target="tpu_custom_call" | custom-call | flops 100000000 | bytes 524288 | tf_op jit(solution)/shard_map/flat_kernel/pallas_call | solution.py:234
  33.6 0.2 collective-permute-done.11.b_ref
  33.9 0.2 collective-permute-done.12.fm_ref
  34.0 0.9 %last_kernel.1 = f32[2,32,512]{2,1,0:T(8,128)} custom-call(f32[2,40,512]{2,1,0:T(8,128)S(1)} %add_add_fusion.1.s_ref, f32[2,40,512]{2,1,0:T(8,128)S(1)} %get-tuple-element.69.n_ref, f32[2,32,512]{2,1,0:T(8,128)S(1)} %collective-permute-done.11.b_ref, f32[2,32,512]{2,1,0:T(8,128)S(1)} %get-tuple-element.64.part_ref, ...), custom_call_target="tpu_custom_call" | custom-call | bytes 131072 | tf_op jit(solution)/shard_map/last_kernel/pallas_call | solution.py:234
  (4 shorter events, 0.1 us)
Async XLA Ops:
  1.8 5.5 %collective-permute-start.1 = (f32[2,40,512]{2,1,0:T(8,128)S(1)}, f32[2,40,512]{2,1,0:T(8,128)S(1)}, u32[]{:S(2)}, u32[]{:S(2)}) collective-permute-start(f32[2,40,512]{2,1,0:T(8,128)S(1)} %get-tuple-element.39), channel_id=1, source_target_pairs={{0,32},{32,0},{64,96},{96,64},{128,160},{160,128},{192,224},{224,1... | collective-permute-start | bytes 491528 | tf_op jit(solution)/shard_map/ppermute | solution.py:271
  4.0 6.9 %collective-permute-start.4 = (f32[2,40,512]{2,1,0:T(8,128)S(1)}, f32[2,40,512]{2,1,0:T(8,128)S(1)}, u32[]{:S(2)}, u32[]{:S(2)}) collective-permute-start(f32[2,40,512]{2,1,0:T(8,128)S(1)} %get-tuple-element.45), channel_id=1, source_target_pairs={{0,192},{32,224},{64,128},{96,160},{128,64},{160,96},{192,0},{224,... | collective-permute-start | bytes 491528 | tf_op jit(solution)/shard_map/ppermute | solution.py:271
  6.5 4.5 %collective-permute-start.5 = (f32[2,40,512]{2,1,0:T(8,128)S(1)}, f32[2,40,512]{2,1,0:T(8,128)S(1)}, u32[]{:S(2)}, u32[]{:S(2)}) collective-permute-start(f32[2,40,512]{2,1,0:T(8,128)S(1)} %get-tuple-element.46), channel_id=1, source_target_pairs={{0,64},{32,96},{64,0},{96,32},{128,192},{160,224},{192,128},{224,1... | collective-permute-start | bytes 491528 | tf_op jit(solution)/shard_map/ppermute | solution.py:271
  6.5 9.5 %collective-permute-start = (f32[2,40,512]{2,1,0:T(8,128)S(1)}, f32[2,40,512]{2,1,0:T(8,128)S(1)}, u32[]{:S(2)}, u32[]{:S(2)}) collective-permute-start(f32[2,40,512]{2,1,0:T(8,128)S(1)} %get-tuple-element.38), channel_id=1, source_target_pairs={{0,192},{32,224},{64,128},{96,160},{128,64},{160,96},{192,0},{224,... | collective-permute-start | bytes 491528 | tf_op jit(solution)/shard_map/ppermute | solution.py:271
  7.3 8.7 %collective-permute-start.3 = (f32[2,40,512]{2,1,0:T(8,128)S(1)}, f32[2,40,512]{2,1,0:T(8,128)S(1)}, u32[]{:S(2)}, u32[]{:S(2)}) collective-permute-start(f32[2,40,512]{2,1,0:T(8,128)S(1)} %add.31), channel_id=1, source_target_pairs={{0,128},{32,160},{64,192},{96,224},{128,0},{160,32},{192,64},{224,... | collective-permute-start | bytes 491528 | tf_op jit(solution)/shard_map/ppermute | solution.py:271
  10.6 7.6 %collective-permute-start.2 = (f32[2,40,512]{2,1,0:T(8,128)S(1)}, f32[2,40,512]{2,1,0:T(8,128)S(1)}, u32[]{:S(2)}, u32[]{:S(2)}) collective-permute-start(f32[2,40,512]{2,1,0:T(8,128)S(1)} %get-tuple-element.41), channel_id=1, source_target_pairs={{0,64},{32,96},{64,0},{96,32},{128,192},{160,224},{192,128},{224,1... | collective-permute-start | bytes 491528 | tf_op jit(solution)/shard_map/ppermute | solution.py:271
  11.0 7.3 %collective-permute-start.6 = (f32[2,40,512]{2,1,0:T(8,128)S(1)}, f32[2,40,512]{2,1,0:T(8,128)S(1)}, u32[]{:S(2)}, u32[]{:S(2)}) collective-permute-start(f32[2,40,512]{2,1,0:T(8,128)S(1)} %add_add_fusion), channel_id=1, source_target_pairs={{0,32},{32,0},{64,96},{96,64},{128,160},{160,128},{192,224},{224,1... | collective-permute-start | bytes 491528 | tf_op jit(solution)/shard_map/ppermute | solution.py:271
  18.3 11.7 %collective-permute-start.9 = (f32[2,40,512]{2,1,0:T(8,128)S(1)}, f32[2,40,512]{2,1,0:T(8,128)S(1)}, u32[]{:S(2)}, u32[]{:S(2)}) collective-permute-start(f32[2,40,512]{2,1,0:T(8,128)S(1)} %add_add_fusion.1.s_ref), channel_id=1, source_target_pairs={{0,3},{1,2},{2,1},{3,0},{4,4},{5,5},{6,6},{7,7},{8,8},{9,9},{10,10... | collective-permute-start | bytes 491528 | tf_op jit(solution)/shard_map/ppermute | solution.py:287
  23.6 8.4 %collective-permute-start.8 = (f32[2,40,512]{2,1,0:T(8,128)S(1)}, f32[2,40,512]{2,1,0:T(8,128)S(1)}, u32[]{:S(2)}, u32[]{:S(2)}) collective-permute-start(f32[2,40,512]{2,1,0:T(8,128)S(1)} %add_add_fusion.1.s_ref), channel_id=1, source_target_pairs={{0,31},{1,30},{2,5},{3,4},{4,3},{5,2},{6,9},{7,8},{8,7},{9,6},{10,... | collective-permute-start | bytes 491528 | tf_op jit(solution)/shard_map/ppermute | solution.py:288
  28.8 3.3 %collective-permute-start.7 = (f32[2,40,512]{2,1,0:T(8,128)S(1)}, f32[2,40,512]{2,1,0:T(8,128)S(1)}, u32[]{:S(2)}, u32[]{:S(2)}) collective-permute-start(f32[2,40,512]{2,1,0:T(8,128)S(1)} %add_add_fusion.1.s_ref), channel_id=1, source_target_pairs={{0,0},{1,1},{2,2},{3,3},{4,7},{5,6},{6,5},{7,4},{8,11},{9,10},{10,... | collective-permute-start | bytes 491528 | tf_op jit(solution)/shard_map/ppermute | solution.py:289
  29.5 2.7 %collective-permute-start.10 = (f32[2,40,512]{2,1,0:T(8,128)S(1)}, f32[2,40,512]{2,1,0:T(8,128)S(1)}, u32[]{:S(2)}, u32[]{:S(2)}) collective-permute-start(f32[2,40,512]{2,1,0:T(8,128)S(1)} %add_add_fusion.1.s_ref), channel_id=1, source_target_pairs={{0,1},{1,0},{2,3},{3,2},{4,5},{5,4},{6,7},{7,6},{8,9},{9,8},{10,11... | collective-permute-start | bytes 491528 | tf_op jit(solution)/shard_map/ppermute | solution.py:290
  32.4 1.4 %collective-permute-start.11 = (f32[2,32,512]{2,1,0:T(8,128)S(1)}, f32[2,32,512]{2,1,0:T(8,128)S(1)}, u32[]{:S(2)}, u32[]{:S(2)}) collective-permute-start(f32[2,32,512]{2,1,0:T(8,128)S(1)} %slice_select_fusion), channel_id=1, source_target_pairs={{0,1},{1,0},{2,3},{3,2},{4,5},{5,4},{6,7},{7,6},{8,9},{9,8},{10,11... | collective-permute-start | bytes 393224 | tf_op jit(solution)/shard_map/ppermute | solution.py:304
  32.5 1.5 %collective-permute-start.12 = (f32[2,32,512]{2,1,0:T(8,128)S(1)}, f32[2,32,512]{2,1,0:T(8,128)S(1)}, u32[]{:S(2)}, u32[]{:S(2)}) collective-permute-start(f32[2,32,512]{2,1,0:T(8,128)S(1)} %get-tuple-element.57.fz_ref), channel_id=1, source_target_pairs={{0,1},{1,0},{2,3},{3,2},{4,5},{5,4},{6,7},{7,6},{8,9},{9,8},{10,11... | collective-permute-start | bytes 393224 | tf_op jit(solution)/shard_map/ppermute | solution.py:305
